TPU v7x, 32 devices: a whole 2x2x4 slice. The times are simulated.
32 devices in a mesh: gx: 4 (over z), gy: 8 (over y, x, core).
Axes of the slice: x: 2, y: 2, z: 4, core: 2. Of those that a mesh axis runs over, the one named last changes fastest.
Arguments:
- board_activations_input: bfloat16 [128, 19, 19, 256], P(('gx', 'gy')), may hold values from -14 to 14
- conv1_weight: bfloat16 [9, 256, 256], P(None, ('gx', 'gy')), may hold values from -0.125 to 0.125
- conv2_weight: bfloat16 [9, 256, 256], P(None, ('gx', 'gy')), may hold values from -0.125 to 0.125
- norm_gains: bfloat16 [2, 256], P(None, ('gx', 'gy')), may hold values from 0.5 to 1.5
- norm_shifts: bfloat16 [2, 256], P(None, ('gx', 'gy')), may hold values from -1.5 to 1.5
- head_conv: bfloat16 [2, 256], P(None, ('gx', 'gy')), may hold values from -0.375 to 0.375
- head_norm_gain: float32 [2], replicated, may hold values from 0.5 to 1.5
- head_norm_shift: float32 [2], replicated, may hold values from -2 to 2
- dense_weight: bfloat16 [736, 362], P(('gx', 'gy')), may hold values from -0.4375 to 0.4375
- legal_moves: int32 [128, 362], P(('gx', 'gy')), may hold values from 0 to 1, as said below
- target_moves: int32 [128], P(('gx', 'gy')), may hold values from 0 to 361, as said below
- out_cotangent: bfloat16 [128, 19, 19, 256], P(('gx', 'gy')), may hold values from -0.35 to 0.35
Outputs:
- block_output: bfloat16 [128, 19, 19, 256], P(('gx', 'gy'))
- policy_loss: float32 [], replicated
- input_grad: bfloat16 [128, 19, 19, 256], P(('gx', 'gy'))
- conv1_grad: float32 [9, 256, 256], P(None, ('gx', 'gy'))
- conv2_grad: float32 [9, 256, 256], P(None, ('gx', 'gy'))
- gains_grad: float32 [2, 256], P(None, ('gx', 'gy'))
- shifts_grad: float32 [2, 256], P(None, ('gx', 'gy'))
- head_conv_grad: float32 [2, 256], P(None, ('gx', 'gy'))
- head_norm_grad: float32 [2, 2], replicated
- dense_grad: float32 [736, 362], P(('gx', 'gy'))
Inputs may be any that keep to these rules, and one draw needn't show every extreme that they name: `legal_moves`: the pass, move 362 - 1, is legal in every position; the number of legal moves differs from position to position. `target_moves`: A legal move of its position.
All inputs are finite; a program needn't handle non-finite values.
Results may differ from a plain program's by a relative error of at most 0.011.
Values may be sent and summed in bfloat16 or wider, within the bound.
A program may use at most 64 MiB of HBM per device.

v0:
```python
import jax
import jax.numpy as jnp
from jax import lax
from jax.sharding import PartitionSpec as P

epsilon = 1e-05
negative_fill = -1e30
layout = ("NHWC", "HWIO", "NHWC")


def filters_of(kernel):
    return kernel.reshape(3, 3, kernel.shape[1], kernel.shape[2])


def flipped(kernel):
    return jnp.transpose(filters_of(kernel)[::-1, ::-1], (0, 1, 3, 2))


def convolve(planes, filters):
    return lax.conv_general_dilated(
        planes,
        filters,
        (1, 1),
        "SAME",
        dimension_numbers=layout,
        preferred_element_type=jnp.float32,
    )


def kernel_grad(planes, gradient):
    board_side = planes.shape[1]
    padded = jnp.pad(planes, ((0, 0), (1, 1), (1, 1), (0, 0)))
    grad_rows = gradient.reshape(-1, gradient.shape[3])
    tap_terms = []
    for vertical in range(3):
        for lateral in range(3):
            window = padded[
                :, vertical : vertical + board_side, lateral : lateral + board_side, :
            ].reshape(-1, planes.shape[3])
            tap_terms.append(
                lax.dot_general(
                    window, grad_rows, (((0,), (0,)), ((), ())), preferred_element_type=jnp.float32
                )
            )
    return jnp.stack(tap_terms)


def norm_stats(values, over_axes, board_cell_count):
    totals = lax.psum(jnp.sum(values, axis=over_axes, keepdims=True), ("gx", "gy"))
    center = totals / board_cell_count
    deviation = values - center
    squares = lax.psum(jnp.sum(deviation * deviation, axis=over_axes, keepdims=True), ("gx", "gy"))
    spread = squares / board_cell_count
    return (center, lax.rsqrt(spread + epsilon))


def norm_gradient_sums(upstream, normed, over_axes):
    return lax.psum(
        (
            jnp.sum(upstream * normed, axis=over_axes, keepdims=True),
            jnp.sum(upstream, axis=over_axes, keepdims=True),
        ),
        ("gx", "gy"),
    )


def gelu_back(inputs, upstream):
    return jax.vjp(jax.nn.gelu, inputs)[1](upstream)[0]


def body(
    board_activations_input,
    conv1_weight,
    conv2_weight,
    norm_gains,
    norm_shifts,
    head_conv,
    head_norm_gain,
    head_norm_shift,
    dense_weight,
    legal_moves,
    target_moves,
    out_cotangent,
):
    first_kernel, second_kernel, gain_rows, shift_rows, head_kernel, dense_full = (
        lax.all_gather(conv1_weight, ("gx", "gy"), axis=1, tiled=True),
        lax.all_gather(conv2_weight, ("gx", "gy"), axis=1, tiled=True),
        lax.all_gather(norm_gains, ("gx", "gy"), axis=1, tiled=True),
        lax.all_gather(norm_shifts, ("gx", "gy"), axis=1, tiled=True),
        lax.all_gather(head_conv, ("gx", "gy"), axis=1, tiled=True),
        lax.all_gather(dense_weight, ("gx", "gy"), axis=0, tiled=True),
    )
    positions = board_activations_input.shape[0]
    board_side = board_activations_input.shape[1]
    channels = board_activations_input.shape[3]
    head_channels = head_conv.shape[0]
    devices = lax.axis_size(("gx", "gy"))
    pixels = board_side * board_side
    board_cell_count = float(positions * pixels * devices)
    gain_parameters = gain_rows.astype(jnp.float32)
    shift_parameters = shift_rows.astype(jnp.float32)
    first_preactivation = convolve(board_activations_input, filters_of(first_kernel))
    first_centered_input, first_inverse_deviation = norm_stats(
        first_preactivation, (0, 1, 2), board_cell_count
    )
    first_standardized = (first_preactivation - first_centered_input) * first_inverse_deviation
    first_normalized_output = first_standardized * gain_parameters[0] + shift_parameters[0]
    first_act = jax.nn.gelu(first_normalized_output).astype(jnp.bfloat16)
    second_preactivation = convolve(first_act, filters_of(second_kernel))
    second_centered_input, second_inverse_deviation = norm_stats(
        second_preactivation, (0, 1, 2), board_cell_count
    )
    second_standardized = (second_preactivation - second_centered_input) * second_inverse_deviation
    residual_sum = (
        board_activations_input.astype(jnp.float32)
        + second_standardized * gain_parameters[1]
        + shift_parameters[1]
    )
    output = jax.nn.gelu(residual_sum).astype(jnp.bfloat16)
    out_rows = output.reshape(-1, channels)
    head_preactivation = lax.dot_general(
        head_kernel, out_rows, (((1,), (1,)), ((), ())), preferred_element_type=jnp.float32
    )
    head_centered_input, head_inverse_deviation = norm_stats(
        head_preactivation, (1,), board_cell_count
    )
    head_standardized = (head_preactivation - head_centered_input) * head_inverse_deviation
    head_normalized_output = head_standardized * head_norm_gain[:, None] + head_norm_shift[:, None]
    features = jax.nn.gelu(head_normalized_output).astype(jnp.bfloat16)
    head_flat = jnp.transpose(
        features.reshape(head_channels, positions, pixels), (1, 0, 2)
    ).reshape(positions, -1)
    head_inputs = head_flat.shape[1]
    logits = jnp.dot(
        head_flat, dense_full[:head_inputs], preferred_element_type=jnp.float32
    ) + dense_full[head_inputs].astype(jnp.float32)
    is_legal = legal_moves == 1
    masked = jnp.where(is_legal, logits, negative_fill)
    row_top = jnp.max(masked, axis=1, keepdims=True)
    exp_terms = jnp.exp(masked - row_top)
    exp_total = jnp.sum(exp_terms, axis=1, keepdims=True)
    log_total = row_top + jnp.log(exp_total)
    move_index = lax.broadcasted_iota(jnp.int32, logits.shape, 1)
    chosen = move_index == target_moves[:, None]
    picked = jnp.sum(jnp.where(chosen, logits, 0.0), axis=1, keepdims=True)
    mean_loss = lax.psum(jnp.sum(log_total - picked), ("gx", "gy")) / float(positions * devices)
    (
        first_back_kernel,
        second_back_kernel,
        gain_back_rows,
        shift_unused,
        head_back_kernel,
        dense_back,
    ) = (
        lax.all_gather(conv1_weight, ("gx", "gy"), axis=1, tiled=True),
        lax.all_gather(conv2_weight, ("gx", "gy"), axis=1, tiled=True),
        lax.all_gather(norm_gains, ("gx", "gy"), axis=1, tiled=True),
        lax.all_gather(norm_shifts, ("gx", "gy"), axis=1, tiled=True),
        lax.all_gather(head_conv, ("gx", "gy"), axis=1, tiled=True),
        lax.all_gather(dense_weight, ("gx", "gy"), axis=0, tiled=True),
    )
    gain_back = gain_back_rows.astype(jnp.float32)
    logit_grad = (exp_terms / exp_total - chosen.astype(jnp.float32)).astype(jnp.bfloat16)
    dense_main = lax.dot_general(
        head_flat, logit_grad, (((0,), (0,)), ((), ())), preferred_element_type=jnp.float32
    )
    dense_bias = jnp.sum(logit_grad.astype(jnp.float32), axis=0, keepdims=True)
    unused_rows = jnp.zeros(
        (dense_full.shape[0] - head_inputs - 1, dense_full.shape[1]), jnp.float32
    )
    dense_term = jnp.concatenate([dense_main, dense_bias, unused_rows], axis=0)
    flat_grad = lax.dot_general(
        logit_grad,
        dense_back[:head_inputs],
        (((1,), (1,)), ((), ())),
        preferred_element_type=jnp.float32,
    )
    feature_grad = jnp.transpose(
        flat_grad.reshape(positions, head_channels, pixels), (1, 0, 2)
    ).reshape(head_channels, -1)
    head_incoming_gradient = gelu_back(head_normalized_output, feature_grad)
    head_gain_gradient_sum, head_shift_gradient_sum = norm_gradient_sums(
        head_incoming_gradient, head_standardized, (1,)
    )
    head_back = (
        head_norm_gain[:, None]
        * head_inverse_deviation
        * (
            head_incoming_gradient
            - (head_shift_gradient_sum + head_standardized * head_gain_gradient_sum)
            / board_cell_count
        )
    ).astype(jnp.bfloat16)
    out_back = lax.dot_general(
        head_back, head_back_kernel, (((0,), (0,)), ((), ())), preferred_element_type=jnp.float32
    )
    head_kernel_term = lax.dot_general(
        head_back, out_rows, (((1,), (0,)), ((), ())), preferred_element_type=jnp.float32
    )
    upstream = out_cotangent.astype(jnp.float32) + out_back.reshape(board_activations_input.shape)
    residual_sum_gradient = gelu_back(residual_sum, upstream)
    second_gain_gradient_sum, second_shift_gradient_sum = norm_gradient_sums(
        residual_sum_gradient, second_standardized, (0, 1, 2)
    )
    second_back = (
        gain_back[1]
        * second_inverse_deviation
        * (
            residual_sum_gradient
            - (second_shift_gradient_sum + second_standardized * second_gain_gradient_sum)
            / board_cell_count
        )
    ).astype(jnp.bfloat16)
    second_term = kernel_grad(first_act, second_back)
    first_incoming_gradient = gelu_back(
        first_normalized_output, convolve(second_back, flipped(second_back_kernel))
    )
    first_gain_gradient_sum, first_shift_gradient_sum = norm_gradient_sums(
        first_incoming_gradient, first_standardized, (0, 1, 2)
    )
    first_back = (
        gain_back[0]
        * first_inverse_deviation
        * (
            first_incoming_gradient
            - (first_shift_gradient_sum + first_standardized * first_gain_gradient_sum)
            / board_cell_count
        )
    ).astype(jnp.bfloat16)
    first_term = kernel_grad(board_activations_input, first_back)
    input_grad = (residual_sum_gradient + convolve(first_back, flipped(first_back_kernel))).astype(
        jnp.bfloat16
    )
    first_share, second_share, head_share, dense_share = (
        lax.psum_scatter(first_term, ("gx", "gy"), scatter_dimension=1, tiled=True),
        lax.psum_scatter(second_term, ("gx", "gy"), scatter_dimension=1, tiled=True),
        lax.psum_scatter(head_kernel_term, ("gx", "gy"), scatter_dimension=1, tiled=True),
        lax.psum_scatter(dense_term, ("gx", "gy"), scatter_dimension=0, tiled=True),
    )
    share_width = channels // devices
    share_start = lax.axis_index(("gx", "gy")) * share_width
    gain_sums = jnp.concatenate(
        [first_gain_gradient_sum.reshape(1, -1), second_gain_gradient_sum.reshape(1, -1)], axis=0
    )
    shift_sums = jnp.concatenate(
        [first_shift_gradient_sum.reshape(1, -1), second_shift_gradient_sum.reshape(1, -1)], axis=0
    )
    gains_grad = lax.dynamic_slice_in_dim(gain_sums, share_start, share_width, 1)
    shifts_grad = lax.dynamic_slice_in_dim(shift_sums, share_start, share_width, 1)
    head_norm_grad = jnp.stack([head_gain_gradient_sum[:, 0], head_shift_gradient_sum[:, 0]])
    return (
        output,
        mean_loss,
        input_grad,
        first_share,
        second_share,
        gains_grad,
        shifts_grad,
        head_share,
        head_norm_grad,
        dense_share,
    )


def solution(mesh):
    return jax.shard_map(
        body,
        mesh=mesh,
        in_specs=(
            P(("gx", "gy"), None, None, None),
            P(None, ("gx", "gy"), None),
            P(None, ("gx", "gy"), None),
            P(None, ("gx", "gy")),
            P(None, ("gx", "gy")),
            P(None, ("gx", "gy")),
            P(),
            P(),
            P(("gx", "gy"), None),
            P(("gx", "gy"), None),
            P(("gx", "gy")),
            P(("gx", "gy"), None, None, None),
        ),
        out_specs=(
            P(("gx", "gy"), None, None, None),
            P(),
            P(("gx", "gy"), None, None, None),
            P(None, ("gx", "gy"), None),
            P(None, ("gx", "gy"), None),
            P(None, ("gx", "gy")),
            P(None, ("gx", "gy")),
            P(None, ("gx", "gy")),
            P(),
            P(("gx", "gy"), None),
        ),
        check_vma=False,
    )
```

profile of v0, /device:TPU:0, one launch (start us, length us, event | category | flops | bytes accessed | tf_op | source)
XLA Modules:
  0.0 919.8 jit_solution(15744320302789858815)
XLA Ops:
  8.7 45.1 %all-gather.3 = bf16[32,23,362]{2,1,0:T(8,128)(2,1)S(1)} all-gather(bf16[1,23,362]{2,1,0:T(8,128)(2,1)} %bitcast.333), channel_id=1, replica_groups=mesh['gx'=4,'gy'=8] {'gx','gy'}, dimensions={0}, use_global_device_ids=true | all-gather | bytes 549516 | tf_op jit(solution)/shard_map/all_gather | solution.py:91
  54.8 36.6 %all-gather = bf16[32,8,2]{1,2,0:T(2,128)(2,1)S(1)} all-gather(bf16[1,8,2]{1,2,0:T(2,128)(2,1)} %bitcast.381), channel_id=1, replica_groups=mesh['gx'=4,'gy'=8] {'gx','gy'}, dimensions={0}, use_global_device_ids=true | all-gather | bytes 1056 | tf_op jit(solution)/shard_map/all_gather | solution.py:88
  94.5 37.8 %all-gather.1 = bf16[32,8,2]{1,2,0:T(2,128)(2,1)S(1)} all-gather(bf16[1,8,2]{1,2,0:T(2,128)(2,1)S(1)} %bitcast.382), channel_id=1, replica_groups=mesh['gx'=4,'gy'=8] {'gx','gy'}, dimensions={0}, use_global_device_ids=true | all-gather | bytes 1056 | tf_op jit(solution)/shard_map/all_gather | solution.py:89
  132.5 36.5 %all-gather.2 = bf16[32,8,2]{1,2,0:T(2,128)(2,1)S(1)} all-gather(bf16[1,8,2]{1,2,0:T(2,128)(2,1)S(1)} %bitcast.383), channel_id=1, replica_groups=mesh['gx'=4,'gy'=8] {'gx','gy'}, dimensions={0}, use_global_device_ids=true | all-gather | bytes 1056 | tf_op jit(solution)/shard_map/all_gather | solution.py:90
  170.8 4.5 select_reduce_fusion.5
  175.3 37.2 %psum.91 = f32[1,1,1,256]{3,2,1,0:T(1,128)S(1)} all-reduce(f32[1,1,1,256]{3,2,1,0:T(1,128)} %bitcast.375), channel_id=1, replica_groups=mesh['gx'=4,'gy'=8] {'gx','gy'}, use_global_device_ids=true, to_apply=%region_1.0 | all-reduce | flops 256 | bytes 2048 | tf_op jit(solution)/shard_map/psum | solution.py:49
  213.6 42.4 %psum.92 = f32[1,1,1,256]{3,2,1,0:T(1,128)S(1)} all-reduce(f32[1,1,1,256]{3,2,1,0:T(1,128)S(1)} %bitcast.348), channel_id=1, replica_groups=mesh['gx'=4,'gy'=8] {'gx','gy'}, use_global_device_ids=true, to_apply=%region_3.0 | all-reduce | flops 256 | bytes 2048 | tf_op jit(solution)/shard_map/psum | solution.py:52
  260.2 4.5 select_reduce_fusion.3
  264.7 38.5 %psum.93 = f32[1,1,1,256]{3,2,1,0:T(1,128)S(1)} all-reduce(f32[1,1,1,256]{3,2,1,0:T(1,128)} %bitcast.374), channel_id=1, replica_groups=mesh['gx'=4,'gy'=8] {'gx','gy'}, use_global_device_ids=true, to_apply=%region_5.0 | all-reduce | flops 256 | bytes 2048 | tf_op jit(solution)/shard_map/psum | solution.py:49
  304.2 42.2 %psum.94 = f32[1,1,1,256]{3,2,1,0:T(1,128)S(1)} all-reduce(f32[1,1,1,256]{3,2,1,0:T(1,128)S(1)} %bitcast.349), channel_id=1, replica_groups=mesh['gx'=4,'gy'=8] {'gx','gy'}, use_global_device_ids=true, to_apply=%region_7.0 | all-reduce | flops 256 | bytes 2048 | tf_op jit(solution)/shard_map/psum | solution.py:52
  351.4 3.0 reshape.132
  359.9 38.4 %psum.95 = f32[2,1]{0,1:T(1,128)S(1)} all-reduce(f32[2,1]{0,1:T(1,128)S(1)} %bitcast.380), channel_id=1, replica_groups=mesh['gx'=4,'gy'=8] {'gx','gy'}, use_global_device_ids=true, to_apply=%region_9.0 | all-reduce | flops 2 | bytes 16 | tf_op jit(solution)/shard_map/psum | solution.py:49
  398.5 41.6 %psum.96 = f32[2,1]{0,1:T(1,128)S(1)} all-reduce(f32[2,1]{0,1:T(1,128)S(1)} %bitcast.384), channel_id=1, replica_groups=mesh['gx'=4,'gy'=8] {'gx','gy'}, use_global_device_ids=true, to_apply=%region_11.0 | all-reduce | flops 2 | bytes 16 | tf_op jit(solution)/shard_map/psum | solution.py:52
  458.2 38.7 %all-reduce.7 = (f32[2,1]{0,1:T(1,128)}, f32[2,1]{0,1:T(1,128)}) all-reduce(f32[2,1]{0,1:T(1,128)} %bitcast.379, f32[2,1]{0,1:T(1,128)} %bitcast.378), channel_id=1, replica_groups=mesh['gx'=4,'gy'=8] {'gx','gy'}, use_global_device_ids=true, to_apply=%region_20.21 | all-reduce | flops 4 | bytes 32 | tf_op jit(solution)/shard_map/psum | solution.py:58
  501.8 2.8 copy.159
  504.6 4.3 reshape.134
  510.3 3.6 fusion.25
  514.0 42.0 %all-reduce.6 = (f32[1,1,1,256]{3,2,1,0:T(1,128)S(1)}, f32[1,1,1,256]{3,2,1,0:T(1,128)}) all-reduce(f32[1,1,1,256]{3,2,1,0:T(1,128)S(1)} %bitcast.352, f32[1,1,1,256]{3,2,1,0:T(1,128)S(1)} %bitcast.351), channel_id=1, replica_groups=mesh['gx'=4,'gy'=8] {'gx','gy'}, use_global_device_ids=true, to_apply=%region_22.23 | all-reduce | flops 512 | bytes 4096 | tf_op jit(solution)/shard_map/psum | solution.py:58
  560.5 4.2 reshape.136
  569.5 5.8 select_reduce_fusion
  575.3 39.4 %all-reduce.5 = (f32[]{:T(128)}, f32[1,1,1,256]{3,2,1,0:T(1,128)}, f32[1,1,1,256]{3,2,1,0:T(1,128)}, f32[2,256]{1,0:T(2,128)}) all-reduce(f32[]{:T(128)} %subtract_reduce_fusion, f32[1,1,1,256]{3,2,1,0:T(1,128)} %bitcast.377, f32[1,1,1,256]{3,2,1,0:T(1,128)} %bitcast.376, ...), channel_id=1, replica_groups=mesh['gx'=4,'gy'=8] {'gx','gy'}, use_global_device_ids=true, to_apply=%region_16.17 | all-reduce | flops 1025 | bytes 8200 | tf_op jit(solution)/shard_map/psum | solution.py:146
  614.7 3.8 select_bitcast_fusion
  620.4 3.5 reshape.127
  623.9 2.8 fusion.80
  636.4 3.1 copy.169
  639.4 3.5 reshape.113
  658.6 79.4 %fusion = f32[32,362]{1,0:T(8,128)S(1)} fusion(f32[736,362]{1,0:T(8,128)} %maximum_maximum_fusion), kind=kCustom, calls=%all-reduce-scatter | all-reduce-scatter fusion | flops 370689 | bytes 1112064
  744.6 4.1 fusion.41
  751.5 4.3 reshape.138
  760.4 7.4 collective-permute-start.3
  769.8 3.0 collective-permute-start.1
  781.9 129.8 %reduce-scatter.8.cloned.1.call-done = f32[9,8,256]{2,1,0:T(8,128)} async-done(((f32[9,256,256]{2,1,0:T(8,128)}), f32[9,8,256]{2,1,0:T(8,128)}) %reduce-scatter.8.cloned.1.call-update) | async-done | bytes 73744 | tf_op jit(solution)/shard_map/reduce_scatter | solution.py:236
  (216 shorter events, 109.6 us)
Async XLA Ops:
  7.2 84.5 %copy-start.4 = (bf16[4,19,19,256]{3,0,2,1:T(4,128)(2,1)S(1)}, bf16[4,19,19,256]{3,0,2,1:T(4,128)(2,1)}, u32[]{:S(2)}) copy-start(bf16[4,19,19,256]{3,0,2,1:T(4,128)(2,1)} %param.12) | copy-start | bytes 2217988
  7.2 163.6 %all-gather.7.cloned.1.call-start = ((), (), s32[]{:S(2)}) async-start(), calls=%async_computation.2 | async-start | bytes 1216512 | tf_op jit(solution)/shard_map/all_gather | solution.py:86
  7.9 252.3 %all-gather.9.cloned.1.call-start = ((), (), s32[]{:S(2)}) async-start(), calls=%async_computation.3 | async-start | bytes 1216512 | tf_op jit(solution)/shard_map/all_gather | solution.py:87
  8.7 773.2 %reduce-scatter.6.cloned.1.call-start = ((), (), s32[]{:S(2)}) async-start(), calls=%async_computation.4 | async-start | bytes 2433024 | tf_op jit(solution)/shard_map/reduce_scatter | solution.py:235
  54.1 39.3 %copy-start.6 = (bf16[736,362]{1,0:T(8,128)(2,1)}, bf16[736,362]{1,0:T(8,128)(2,1)S(1)}, u32[]{:S(2)}) copy-start(bf16[736,362]{1,0:T(8,128)(2,1)S(1)} %reshape.157) | copy-start | bytes 1598596
  93.3 39.2 %copy-start.46 = (bf16[2,8]{1,0:T(2,128)(2,1)S(1)}, bf16[2,8]{1,0:T(2,128)(2,1)}, u32[]{:S(2)}) copy-start(bf16[2,8]{1,0:T(2,128)(2,1)} %param.17) | copy-start | bytes 100
  93.3 77.5 %copy-start.25 = (pred[32,3]{0,1:T(4,128)(4,1)S(1)}, pred[32,3]{0,1:T(4,128)(4,1)}, u32[]{:S(2)}) copy-start(pred[32,3]{0,1:T(4,128)(4,1)} %constant.98) | copy-start | bytes 292
  170.8 183.6 %copy-start.18 = (f32[1,256]{1,0:T(1,128)}, f32[1,256]{1,0:T(1,128)S(1)}, u32[]{:S(2)}) copy-start(f32[1,256]{1,0:T(1,128)S(1)} %get-tuple-element.85) | copy-start | bytes 3076
  175.3 84.0 %copy-start.1 = (f32[19,32,3,256]{3,1,2,0:T(8,128)}, f32[19,32,3,256]{3,1,2,0:T(8,128)S(1)}, u32[]{:S(2)}) copy-start(f32[19,32,3,256]{3,1,2,0:T(8,128)S(1)} %get-tuple-element.93) | copy-start | bytes 5603332
  212.5 46.8 %copy-start.16 = (f32[1,1,1,256]{3,2,1,0:T(1,128)}, f32[1,1,1,256]{3,2,1,0:T(1,128)S(1)}, u32[]{:S(2)}) copy-start(f32[1,1,1,256]{3,2,1,0:T(1,128)S(1)} %broadcast_multiply_fusion.2) | copy-start | bytes 3076
  264.7 81.7 %copy-start.21 = (f32[1,1,1,256]{3,2,1,0:T(1,128)S(1)}, f32[1,1,1,256]{3,2,1,0:T(1,128)}, u32[]{:S(2)}) copy-start(f32[1,1,1,256]{3,2,1,0:T(1,128)} %copy-done.20) | copy-start | bytes 3076
  264.7 82.3 %copy-start.40 = (f32[1,256]{1,0:T(1,128)S(1)}, f32[1,256]{1,0:T(1,128)}, u32[]{:S(2)}) copy-start(f32[1,256]{1,0:T(1,128)} %get-tuple-element.88) | copy-start | bytes 3076
  355.2 84.9 %copy-start.41 = (f32[2]{0:T(128)S(1)}, f32[2]{0:T(128)}, u32[]{:S(2)}) copy-start(f32[2]{0:T(128)} %param.18) | copy-start | bytes 28
  442.6 59.2 %copy-start.3 = (f32[19,32,3,256]{3,1,2,0:T(8,128)S(1)}, f32[19,32,3,256]{3,1,2,0:T(8,128)}, u32[]{:S(2)}) copy-start(f32[19,32,3,256]{3,1,2,0:T(8,128)} %get-tuple-element.76) | copy-start | bytes 5603332
  496.9 4.3 copy-start.44
  636.3 275.3 %reduce-scatter.8.cloned.1.call-start = ((), (), s32[]{:S(2)}) async-start(), calls=%async_computation.5 | async-start | bytes 2433024 | tf_op jit(solution)/shard_map/reduce_scatter | solution.py:236
  738.0 29.8 %collective-permute-start.7 = (f32[32,362]{1,0:T(8,128)S(1)}, f32[32,362]{1,0:T(8,128)S(1)}, u32[]{:S(2)}, u32[]{:S(2)}) collective-permute-start(f32[32,362]{1,0:T(8,128)S(1)} %fusion), channel_id=1, source_target_pairs={{0,8},{1,9},{2,10},{3,11},{4,12},{5,13},{6,14},{7,15},{8,16},{9,17... | collective-permute-start | bytes 139016
  739.6 30.2 %collective-permute-start.6 = (f32[32,362]{1,0:T(8,128)S(1)}, f32[32,362]{1,0:T(8,128)S(1)}, u32[]{:S(2)}, u32[]{:S(2)}) collective-permute-start(f32[32,362]{1,0:T(8,128)S(1)} %fusion), channel_id=1, source_target_pairs={{0,7},{1,8},{2,9},{3,10},{4,11},{5,12},{6,13},{7,14},{8,15},{9,16}... | collective-permute-start | bytes 139016
  740.9 32.0 %collective-permute-start.5 = (f32[32,362]{1,0:T(8,128)S(1)}, f32[32,362]{1,0:T(8,128)S(1)}, u32[]{:S(2)}, u32[]{:S(2)}) collective-permute-start(f32[32,362]{1,0:T(8,128)S(1)} %fusion), channel_id=1, source_target_pairs={{0,6},{1,7},{2,8},{3,9},{4,10},{5,11},{6,12},{7,13},{8,14},{9,15},... | collective-permute-start | bytes 139016
  742.2 37.0 %collective-permute-start.4 = (f32[32,362]{1,0:T(8,128)S(1)}, f32[32,362]{1,0:T(8,128)S(1)}, u32[]{:S(2)}, u32[]{:S(2)}) collective-permute-start(f32[32,362]{1,0:T(8,128)S(1)} %fusion), channel_id=1, source_target_pairs={{0,5},{1,6},{2,7},{3,8},{4,9},{5,10},{6,11},{7,12},{8,13},{9,14},{... | collective-permute-start | bytes 139016
  751.5 5.7 copy-start.34
  751.5 5.7 copy-start.35
  751.5 5.7 copy-start.38
  751.5 5.7 copy-start.39
  755.7 4.7 collective-permute-start.8
  757.8 17.8 %copy-start.42 = (f32[2,1]{0,1:T(1,128)S(1)}, f32[2,1]{0,1:T(1,128)}, u32[]{:S(2)}) copy-start(f32[2,1]{0,1:T(1,128)} %get-tuple-element.64) | copy-start | bytes 28
  757.8 17.8 %copy-start.43 = (f32[2,1]{0,1:T(1,128)S(1)}, f32[2,1]{0,1:T(1,128)}, u32[]{:S(2)}) copy-start(f32[2,1]{0,1:T(1,128)} %get-tuple-element.65) | copy-start | bytes 28
  760.4 18.8 %copy-start.13 = (f32[23,362]{1,0:T(8,128)}, f32[23,362]{1,0:T(8,128)S(1)}, u32[]{:S(2)}) copy-start(f32[23,362]{1,0:T(8,128)S(1)} %collective-permute-done.8) | copy-start | bytes 99916
  760.4 18.8 %collective-permute-start.3 = (f32[32,362]{1,0:T(8,128)S(1)}, f32[32,362]{1,0:T(8,128)S(1)}, u32[]{:S(2)}, u32[]{:S(2)}) collective-permute-start(f32[32,362]{1,0:T(8,128)S(1)} %fusion), channel_id=1, source_target_pairs={{0,4},{1,5},{2,6},{3,7},{4,8},{5,9},{6,10},{7,11},{8,12},{9,13},{1... | collective-permute-start | bytes 139016
  767.8 11.4 %collective-permute-start.2 = (f32[32,362]{1,0:T(8,128)S(1)}, f32[32,362]{1,0:T(8,128)S(1)}, u32[]{:S(2)}, u32[]{:S(2)}) collective-permute-start(f32[32,362]{1,0:T(8,128)S(1)} %fusion), channel_id=1, source_target_pairs={{0,3},{1,4},{2,5},{3,6},{4,7},{5,8},{6,9},{7,10},{8,11},{9,12},{10... | collective-permute-start | bytes 139016
  769.8 9.4 %collective-permute-start.1 = (f32[32,362]{1,0:T(8,128)S(1)}, f32[32,362]{1,0:T(8,128)S(1)}, u32[]{:S(2)}, u32[]{:S(2)}) collective-permute-start(f32[32,362]{1,0:T(8,128)S(1)} %fusion), channel_id=1, source_target_pairs={{0,2},{1,3},{2,4},{3,5},{4,6},{5,7},{6,8},{7,9},{8,10},{9,11},{10,... | collective-permute-start | bytes 139016
  772.8 6.4 collective-permute-start
  (30 other events, 60.1 us)
Sparse Core Ops, SparseCore 0:
  10.9 56.1 all-gather.6
  70.0 52.4 all-gather.8
  636.5 139.1 reduce-scatter.5
  778.3 133.2 reduce-scatter.7
where the time goes:
time: 930 us; the launch traced here: 920 us
  blocking collectives  596 us (64%)
  waiting for transfers between devices  131 us (14%)
  local copies, waits for them, and re-layouts  68.9 us (7%)
  matrix products  52.8 us (6%)
  other arithmetic  32.2 us (3%)
  starting transfers between devices  22.1 us (2%)
  between operations  16.6 us (2%)
    reduce_scatter x1, waiting for transfers between devices, body(): lax.psum_scatter(second_term, ('gx', 'gy'), scatter_dimension=1, tiled=True)  130 us
    psum x3, blocking collectives, norm_stats(): lax.psum(jnp.sum(deviation * deviation, axis=over_axes, keepdims=True), (...  126 us
    psum x3, blocking collectives, norm_stats(): lax.psum(jnp.sum(values, axis=over_axes, keepdims=True), ('gx', 'gy'))  114 us
    psum x2, blocking collectives, norm_gradient_sums(): lax.psum((jnp.sum(upstream * normed, axis=over_axes, keepdims=True), jnp....  80.7 us
    unnamed x1, blocking collectives  79.4 us
    all_gather x1, blocking collectives, body(): lax.all_gather(dense_weight, ('gx', 'gy'), axis=0, tiled=True)  45.1 us
    psum x1, blocking collectives, body(): lax.psum(jnp.sum(log_total - picked), ('gx', 'gy'))  39.4 us
    all_gather x1, blocking collectives, body(): lax.all_gather(norm_shifts, ('gx', 'gy'), axis=1, tiled=True)  37.8 us
  transfers between devices with their start and end apart: 13, of which 1 were waited for; matrix products, arithmetic and copies ran while one was open for 15% of the time, Pallas kernels for 0%

commit v1 on v0

v1 whole, which is shorter than its diff:
```python
import functools
import types

import jax
import jax.numpy as jnp
from jax import lax
from jax.experimental import pallas as pl
from jax.experimental.pallas import tpu as pltpu
from jax.sharding import PartitionSpec as P

MESH = pl.DeviceIdType.MESH
f32 = jnp.float32
bf16 = jnp.bfloat16
epsilon = 1e-05
negative_fill = -1e30
root = 0.7978845608028654
cube = 0.044715
lanes = 128


def up_to(value, unit):
    return -(-value // unit) * unit


def divided(values, divisor, limit):
    factor = -(-65536 // divisor)
    for n in range(limit):
        assert (n * factor) >> 16 == n // divisor and n * factor < 2**31
    return lax.shift_right_logical(values * factor, jnp.int32(16))


def iota(shape, axis):
    return lax.broadcasted_iota(jnp.int32, shape, axis)


def gelu_both(v):
    square = v * v
    slope = jnp.tanh(v * (root + (root * cube) * square))
    half = 0.5 + 0.5 * slope
    back = half + (0.5 * v) * (1.0 - slope * slope) * (root + (3.0 * root * cube) * square)
    return v * half, back


def dot(left, right):
    return jnp.dot(left, right, preferred_element_type=f32)


def dot_nt(left, right):
    return lax.dot_general(left, right, (((1,), (1,)), ((), ())), preferred_element_type=f32)


def sizes_of(gx_n, gy_n, x, w1, dense, moves):
    s = types.SimpleNamespace()
    s.gx_n, s.gy_n, s.q_n, s.n_dev = gx_n, gy_n, gy_n // 2, gx_n * gy_n
    s.nb, s.side, s.ch = x.shape[0], x.shape[1], x.shape[3]
    s.w = w1.shape[1]
    s.wide = s.side + 1
    s.br = s.wide * s.nb
    s.rows = s.side * s.br
    s.padded = s.rows + 2 * s.br
    s.gap = up_to(s.side, 8)
    s.line = up_to(s.side * s.gap, lanes)
    s.cells = s.side * s.side
    s.moves = moves
    s.mp = up_to(moves, lanes)
    s.rsh = dense.shape[0]
    s.rp = up_to(s.rsh, 16)
    s.head_in = 2 * s.cells
    s.blk = up_to(18 * s.w, 16)
    s.blk1 = up_to(19 * s.w, 16)
    s.fast = s.w == 8
    s.nch = 3 if s.fast else 1
    s.crows = s.blk // s.nch
    s.count = float(s.nb * s.cells * s.n_dev)
    assert s.nb == 4 and s.br % 16 == 0 and gy_n % 2 == 0 and 8 % s.w == 0
    return s


def kernel(s, in_names, out_names, scratch_names, *refs):
    r = types.SimpleNamespace(**dict(zip(in_names + out_names + scratch_names, refs)))
    gx, gy = lax.axis_index("gx"), lax.axis_index("gy")
    q, c = lax.div(gy, 2), lax.rem(gy, 2)
    me = gx * s.gy_n + gy
    other = (gx, gy + 1 - 2 * c)
    gxn, qn, nb, br, gap, ch = s.gx_n, s.q_n, s.nb, s.br, s.gap, s.ch

    def z_peer(k):
        return lax.rem(gx + k, gxn)

    def q_peer(j):
        return lax.rem(q + j, qn)

    def send(src, dst, out_sem, in_sem, device):
        pltpu.make_async_remote_copy(
            src_ref=src, dst_ref=dst, send_sem=out_sem, recv_sem=in_sem, device_id=device, device_id_type=MESH
        ).start()

    def take(sem, ref):
        pltpu.make_async_copy(ref, ref, sem).wait()

    barrier = pltpu.get_barrier_semaphore()
    partners = [(z_peer(k), gy) for k in range(1, gxn)]
    partners += [(gx, 2 * q_peer(j) + c) for j in range(1, qn)]
    partners += [other]
    for p in partners:
        pl.semaphore_signal(barrier, inc=1, device_id=p, device_id_type=MESH)
    fetch_x = pltpu.make_async_copy(r.x, r.x_v, r.local_sem.at[0])
    fetch_x.start()
    fetch_cot = pltpu.make_async_copy(r.cot, r.cot_v, r.local_sem.at[1])
    fetch_cot.start()

    w = s.w

    def stage(weight, rows):
        r.stage[...] = jnp.zeros_like(r.stage)
        for t in range(9):
            v = weight[t].astype(f32)
            r.stage[2 * w * t : 2 * w * t + w, :] = v[:, :lanes]
            r.stage[2 * w * t + w : 2 * w * t + 2 * w, :] = v[:, lanes:]

    r.small[...] = jnp.zeros_like(r.small)
    r.small[0:2, 0:w] = r.gains[...].astype(f32)
    r.small[2:4, 0:w] = r.shifts[...].astype(f32)
    r.small[4:6, 0:w] = r.hc[...].astype(f32)
    stage(r.w1, s.blk1)
    r.stage[18 * w : 19 * w, 0:8] = jnp.transpose(r.small[...])[0:w, :]
    r.s1[gx, q, c] = r.stage[...].astype(bf16)
    stage(r.w2, s.blk)
    r.s2[gx, q, c] = r.stage[0 : s.blk, :].astype(bf16)
    r.dense_v[...] = jnp.zeros_like(r.dense_v)
    r.dense_v[0 : s.rsh, 0 : s.moves] = r.dense[...].astype(f32)
    r.sd[gx, q, c] = r.dense_v[...].astype(bf16)

    for planes in (r.x3, r.a3, r.d3):
        planes[0:br, :] = jnp.zeros((br, 3 * ch), bf16)
        planes[s.padded - br :, :] = jnp.zeros((br, 3 * ch), bf16)
    r.slab[...] = jnp.zeros_like(r.slab)
    r.outp[:, s.side * gap :, :] = jnp.zeros((nb, s.line - s.side * gap, ch), f32)
    row, col = iota((br, nb * gap), 0), iota((br, nb * gap), 1)
    j_of, b_of = lax.shift_right_logical(row, 2), row & 3
    spread = ((col == b_of * gap + j_of) & (j_of < s.side)).astype(f32).astype(bf16)
    row, col = iota((nb * gap, br), 0), iota((nb * gap, br), 1)
    j_of, b_of = lax.shift_right_logical(col, 2), col & 3
    gather_up = ((row == b_of * gap + j_of) & (j_of < s.side)).astype(f32).astype(bf16)
    inside = iota((br, ch), 0) < nb * s.side

    def store3(planes, i, block):
        at = pl.ds(pl.multiple_of((i + 1) * br, 16), br)
        planes[at, 0:ch] = pltpu.roll(block, nb, 0).astype(bf16)
        planes[at, ch : 2 * ch] = block.astype(bf16)
        planes[at, 2 * ch :] = pltpu.roll(block, br - nb, 0).astype(bf16)

    def rows_of(i):
        return pl.ds(pl.multiple_of(i * br, 16), br)

    def to_rows(source, i):
        for b in range(nb):
            r.slab[gap * b : gap * b + s.side, :] = source[b, i].astype(f32)
        return dot(spread, r.slab[...].astype(bf16))

    def x_rows(i, _):
        store3(r.x3, i, to_rows(r.x_v, i))
        return 0

    def cot_rows(i, _):
        r.cot_r[rows_of(i), :] = to_rows(r.cot_v, i).astype(bf16)
        return 0

    fetch_x.wait()
    lax.fori_loop(0, s.side, x_rows, 0)

    pl.semaphore_wait(barrier, len(partners))

    def span(unit):
        store, part = unit
        if store is r.sd:
            return pl.ds(0, s.rp)
        whole = s.blk1 if store is r.s1 else s.blk
        if s.nch == 1:
            return pl.ds(0, whole)
        start = part * s.crows
        return pl.ds(start, whole - start if part == s.nch - 1 else s.crows)

    units = [(r.s1, p) for p in range(s.nch)] + [(r.s2, p) for p in range(s.nch)] + [(r.sd, 0)]

    def g_start(u):
        store, at = units[u][0], span(units[u])
        own = store.at[gx, q, c, at]
        for k in range(gxn - 1, 0, -1):
            send(own, own, r.g_sem.at[u, 0], r.g_sem.at[u, 1], (z_peer(k), gy))
        for j in range(1, qn):
            send(own, own, r.g_sem.at[u, 2], r.g_sem.at[u, 3], (gx, 2 * q_peer(j) + c))

    def g_forward(u):
        store, at = units[u][0], span(units[u])
        take(r.g_sem.at[u, 1], store.at[pl.ds(0, gxn - 1), 0, 0, at])
        for k in range(1, gxn):
            block = store.at[z_peer(k), q, c, at]
            for j in range(1, qn):
                send(block, block, r.g_sem.at[u, 4], r.g_sem.at[u, 3], (gx, 2 * q_peer(j) + c))

    def g_cross(u):
        store, at = units[u][0], span(units[u])
        take(r.g_sem.at[u, 3], store.at[:, pl.ds(0, qn - 1), 0, at])
        block = store.at[:, :, c, at]
        send(block, block, r.g_sem.at[u, 5], r.g_sem.at[u, 6], other)

    def g_done(u):
        store, at = units[u][0], span(units[u])
        take(r.g_sem.at[u, 6], store.at[:, :, 0, at])

    def g_drain(u):
        store, at = units[u][0], span(units[u])
        take(r.g_sem.at[u, 0], store.at[pl.ds(0, gxn - 1), 0, 0, at])
        take(r.g_sem.at[u, 2], store.at[0, pl.ds(0, qn - 1), 0, at])
        take(r.g_sem.at[u, 4], store.at[pl.ds(0, gxn - 1), pl.ds(0, qn - 1), 0, at])
        take(r.g_sem.at[u, 5], store.at[:, :, 0, at])

    def shard_of(store, d):
        return store[lax.div(d, s.gy_n), lax.div(lax.rem(d, s.gy_n), 2), lax.rem(d, 2)]

    def unpack(store, part, weight):
        if s.fast:
            for dj in range(3):
                at = 16 * (3 * part + dj)
                v = store[:, :, :, at : at + 16, :].astype(f32).reshape(s.n_dev, 16, lanes)
                low = v[:, 0:8, :].reshape(ch, lanes)
                high = v[:, 8:16, :].reshape(ch, lanes)
                weight[part, dj * ch : (dj + 1) * ch, :] = jnp.concatenate([low, high], axis=1).astype(bf16)
            return

        def one(g, _):
            for e in range(8 // w):
                r.stage[0 : s.blk, :] = shard_of(store, g * (8 // w) + e)[0 : s.blk].astype(f32)
                for t in range(9):
                    r.eight[t, w * e : w * e + w, 0:lanes] = r.stage[2 * w * t : 2 * w * t + w, :]
                    r.eight[t, w * e : w * e + w, lanes:] = r.stage[2 * w * t + w : 2 * w * t + 2 * w, :]
            for t in range(9):
                r.flat[t, pl.ds(pl.multiple_of(8 * g, 8), 8), :] = r.eight[t]
            return 0

        lax.fori_loop(0, ch // 8, one, 0)
        for t in range(9):
            weight[t // 3, (t % 3) * ch : (t % 3 + 1) * ch, :] = r.flat[t].astype(bf16)

    def unpack_small():
        if s.fast:
            v = r.s1[:, :, :, 18 * w : 18 * w + 16, :].astype(f32).reshape(s.n_dev, 16, lanes)
            rows = v[:, 0:8, :].reshape(ch, lanes)
        else:

            def one(g, _):
                for e in range(8 // w):
                    r.stage[...] = shard_of(r.s1, g * (8 // w) + e).astype(f32)
                    r.eight[0, w * e : w * e + w, 0:lanes] = r.stage[18 * w : 19 * w, :]
                r.flat[0, pl.ds(pl.multiple_of(8 * g, 8), 8), :] = r.eight[0]
                return 0

            lax.fori_loop(0, ch // 8, one, 0)
            rows = r.flat[0, :, 0:lanes]
        r.pars[...] = jnp.transpose(rows)[0:8, :]

    def x_send(number, src, slots):
        def one(n, _):
            k = s.n_dev - 1 - n
            device = (lax.rem(gx + lax.div(k, s.gy_n), gxn), lax.rem(gy + lax.rem(k, s.gy_n), s.gy_n))
            send(src, slots.at[me], r.x_sem.at[number, 0], r.x_sem.at[number, 1], device)
            return 0

        lax.fori_loop(0, s.n_dev - 1, one, 0)
        slots[me] = src[...]

    def x_wait(number, slots):
        take(r.x_sem.at[number, 1], slots.at[pl.ds(0, s.n_dev - 1)])

    def x_drain(number, slots):
        take(r.x_sem.at[number, 0], slots.at[pl.ds(0, s.n_dev - 1)])

    def rs_fill(part, grad, b):
        if s.fast:
            for dj in range(3):
                g = grad[:, (2 - dj) * ch : (3 - dj) * ch]
                low = g[:, :lanes].reshape(s.n_dev, 8, lanes)
                high = g[:, lanes:].reshape(s.n_dev, 8, lanes)
                v = jnp.concatenate([low, high], axis=1).astype(bf16).reshape(gxn, qn, 2, 16, lanes)
                for core in range(2):
                    b.rsb[part, core, :, :, 16 * dj : 16 * dj + 16, :] = v[:, :, core]
        else:
            for dj in range(3):
                r.flat[3 * part + dj] = grad[:, (2 - dj) * ch : (3 - dj) * ch]

    def rs_fill_rest(b):
        if s.fast:
            return
        r.stage[...] = jnp.zeros_like(r.stage)

        def one(g, _):
            for t in range(9):
                r.eight[t] = r.flat[t, pl.ds(pl.multiple_of(8 * g, 8), 8), :]
            for e in range(8 // w):
                d = g * (8 // w) + e
                for t in range(9):
                    v = r.eight[t, w * e : w * e + w, :]
                    r.stage[2 * w * t : 2 * w * t + w, :] = v[:, :lanes]
                    r.stage[2 * w * t + w : 2 * w * t + 2 * w, :] = v[:, lanes:]
                at = (0, lax.rem(d, 2), lax.div(d, s.gy_n), lax.div(lax.rem(d, s.gy_n), 2))
                b.rsb[at] = r.stage[0 : s.blk, :].astype(bf16)
            return 0

        lax.fori_loop(0, ch // 8, one, 0)

    def rs_cross(b, part):
        send(b.rsb.at[part, 1 - c], b.rc.at[part], b.sem.at[part, 0], b.sem.at[part, 1], other)

    def rs_plane(b, part):
        take(b.sem.at[part, 1], b.rc.at[part])
        for p in range(qn):
            total = b.rsb[part, c, :, p].astype(f32) + b.rc[part, :, p].astype(f32)
            b.pb[part, p] = total.astype(bf16)
        for j in range(1, qn):
            to = q_peer(j)
            send(b.pb.at[part, to], b.rp.at[part, j - 1], b.sem.at[part, 2], b.sem.at[part, 3], (gx, 2 * to + c))

    def rs_line(b, part):
        take(b.sem.at[part, 3], b.rp.at[part])
        total = b.pb[part, q].astype(f32)
        for j in range(qn - 1):
            total = total + b.rp[part, j].astype(f32)
        b.zb[part] = total.astype(bf16)
        for k in range(1, gxn):
            to = z_peer(k)
            send(b.zb.at[part, to], b.rz.at[part, k - 1], b.sem.at[part, 4], b.sem.at[part, 5], (to, gy))

    def rs_finish(b, part, out):
        take(b.sem.at[part, 5], b.rz.at[part])
        total = b.zb[part, gx].astype(f32)
        for k in range(gxn - 1):
            total = total + b.rz[part, k].astype(f32)
        taps = 9 // s.nch
        for t in range(taps):
            at = 2 * w * t
            out[part * taps + t] = jnp.concatenate([total[at : at + w], total[at + w : at + 2 * w]], axis=1)

    def rs_drain(b):
        for part in range(s.nch):
            take(b.sem.at[part, 0], b.rc.at[part])
            take(b.sem.at[part, 2], b.rp.at[part])
            take(b.sem.at[part, 4], b.rz.at[part])

    def rs_buffers(number):
        names = ("rsb", "rc", "pb", "rp", "zb", "rz")
        b = types.SimpleNamespace(**{n: getattr(r, n + number) for n in names})
        b.sem = getattr(r, "rs_sem" + number)
        return b

    rs1, rs2 = rs_buffers("1"), rs_buffers("2")

    def local_stats(field, out):
        pivot = field[0:1, :]

        def one(i, carry):
            d = jnp.where(inside, field[rows_of(i), :] - pivot, 0.0).reshape(br // 8, 8, ch)
            return carry[0] + jnp.sum(d, axis=0), carry[1] + jnp.sum(d * d, axis=0)

        zero = jnp.zeros((8, ch), f32)
        first, second = lax.fori_loop(0, s.side, one, (zero, zero))
        n = float(nb * s.cells)
        first = jnp.sum(first, axis=0, keepdims=True) / n
        second = jnp.sum(second, axis=0, keepdims=True) - n * first * first
        out[0:1, :] = pivot + first
        out[1:2, :] = second

    def global_stats(slots):
        v = slots[...]
        n = float(nb * s.cells)
        mean = jnp.sum(v[:, 0:1, :], axis=0) / s.n_dev
        d = v[:, 0:1, :] - mean
        spread_sum = jnp.sum(v[:, 1:2, :] + n * d * d, axis=0)
        return mean, lax.rsqrt(spread_sum / s.count + epsilon)

    n1 = s.nch
    for u in range(n1):
        g_start(u)
    for u in range(n1):
        g_forward(u)
    for u in range(n1, len(units)):
        g_start(u)
    fetch_cot.wait()
    lax.fori_loop(0, s.side, cot_rows, 0)
    r.xt[...] = jnp.transpose(r.x3[br : br + s.rows, ch : 2 * ch])
    for u in range(n1):
        g_cross(u)
    for u in range(n1, 2 * n1):
        g_forward(u)

    def conv_part(planes, weight, di, out):
        v = dot(planes[br * di : br * di + s.rows, :], weight[di])
        out[...] = v if di == 0 else out[...] + v

    def conv(planes, weight, out):
        v = dot(planes[0 : s.rows, :], weight[0])
        v = v + dot(planes[br : br + s.rows, :], weight[1])
        out[...] = v + dot(planes[2 * br : 2 * br + s.rows, :], weight[2])

    for part in range(n1):
        g_done(part)
        unpack(r.s1, part, r.wt1)
        if s.fast:
            conv_part(r.x3, r.wt1, part, r.h1)
    if not s.fast:
        conv(r.x3, r.wt1, r.h1)
    local_stats(r.h1, r.st1)
    x_send(0, r.st1, r.t1)

    unpack_small()
    for u in range(n1, 2 * n1):
        g_cross(u)
    g_forward(2 * n1)

    def flip(weight, back):
        for di in range(3):
            for dj in range(3):
                tap = weight[2 - di, (2 - dj) * ch : (3 - dj) * ch, :]
                back[di, dj * ch : (dj + 1) * ch, :] = jnp.transpose(tap)

    flip(r.wt1, r.wb1)
    for u in range(n1, 2 * n1):
        g_done(u)
        unpack(r.s2, u - n1, r.wt2)

    gain1, gain2 = r.pars[0:1, :], r.pars[1:2, :]
    shift1, shift2 = r.pars[2:3, :], r.pars[3:4, :]
    hc0, hc1 = r.pars[4:5, :], r.pars[5:6, :]

    x_wait(0, r.t1)
    mean1, inv1 = global_stats(r.t1)

    def act1(i, _):
        n = (r.h1[rows_of(i), :] - mean1) * (inv1 * gain1) + shift1
        a, back = gelu_both(n)
        r.back1[rows_of(i), :] = back
        store3(r.a3, i, jnp.where(inside, a, 0.0))
        return 0

    lax.fori_loop(0, s.side, act1, 0)
    conv(r.a3, r.wt2, r.h2)
    local_stats(r.h2, r.st2)
    x_send(1, r.st2, r.t2)

    r.at[...] = jnp.transpose(r.a3[br : br + s.rows, ch : 2 * ch])
    flip(r.wt2, r.wb2)
    g_cross(2 * n1)
    g_done(2 * n1)
    at = iota((s.line, 1), 0)
    i_of = divided(at, gap, s.line)
    j_of = at - i_of * gap
    used = (i_of < s.side) & (j_of < s.side)
    wide_slots = s.n_dev * s.rp
    shard_rows = iota((s.line, wide_slots), 1)
    dense_all = r.sd[...].reshape(wide_slots, s.mp)
    for k in range(2):
        source = k * s.cells + i_of * s.side + j_of
        if k == 0:
            source = jnp.where(at == s.side, s.head_in, source)
            wanted = used | (at == s.side)
        else:
            wanted = used
        source = jnp.where(wanted, source, 0)
        shard = divided(source, s.rsh, 1024)
        place = jnp.where(wanted, shard * s.rp + (source - shard * s.rsh), -1)
        pick = (shard_rows == place).astype(f32).astype(bf16)
        r.dk[k] = dot(pick, dense_all).astype(bf16)
    row, col = iota((s.rows, s.line), 0), iota((s.rows, s.line), 1)
    row_line = lax.shift_right_logical(iota((s.rows, 1), 0), 2)
    row_i = divided(row_line, s.wide, s.rows // nb)
    row_at = row_i * gap + (row_line - row_i * s.wide)
    r.expand[...] = (col == row_at).astype(f32).astype(bf16)
    r.dp_full[...] = jnp.zeros_like(r.dp_full)
    r.hc_full[...] = jnp.zeros_like(r.hc_full)
    row = iota((16, ch), 0)
    both = jnp.where(row < nb, hc0, jnp.where(row < 2 * nb, hc1, 0.0))
    r.hc_full[0:16, :] = both.astype(bf16)

    x_wait(1, r.t2)
    mean2, inv2 = global_stats(r.t2)

    def act2(i, _):
        at = rows_of(i)
        xin = r.x3[pl.ds(pl.multiple_of((i + 1) * br, 16), br), ch : 2 * ch].astype(f32)
        z = xin + ((r.h2[at, :] - mean2) * (inv2 * gain2) + shift2)
        a, back = gelu_both(z)
        r.dz[at, :] = back
        up = dot(gather_up, jnp.where(inside, a, 0.0).astype(bf16))
        for b in range(nb):
            r.outp[b, pl.ds(pl.multiple_of(i * gap, 8), gap), :] = up[gap * b : gap * b + gap]
            r.out[b, i] = up[gap * b : gap * b + s.side].astype(bf16)
        return 0

    lax.fori_loop(0, s.side, act2, 0)
    row = iota((8, s.line), 0)
    lane = iota((8, s.line), 1)
    lane_i = divided(lane, gap, s.line)
    valid = (lane_i < s.side) & (lane - lane_i * gap < s.side)
    first_head = row < nb
    row256 = iota((16, ch), 0)
    p8 = jnp.zeros((8, s.line), f32)
    for b in range(nb):
        head = jnp.where(row256 == b, hc0, jnp.where(row256 == nb + b, hc1, 0.0)).astype(bf16)
        p8 = p8 + dot_nt(head, r.outp[b].astype(bf16))[0:8]

    row1, lane1 = iota((8, lanes), 0), iota((8, lanes), 1)

    def by_head(v):
        a = v[0:1] + v[1:2] + v[2:3] + v[3:4]
        b = v[4:5] + v[5:6] + v[6:7] + v[7:8]
        return jnp.where(iota(v.shape, 0) < nb, a, b)

    cells = float(s.cells)
    mean_row = jnp.sum(jnp.where(valid, p8, 0.0), axis=1, keepdims=True) / cells
    dev = jnp.where(valid, p8 - mean_row, 0.0)
    square_row = jnp.sum(dev * dev, axis=1, keepdims=True)
    r.st3[...] = jnp.where(lane1 < 64, mean_row, square_row)
    x_send(2, r.st3, r.t3)
    x_wait(2, r.t3)
    v = r.t3[...]
    mean_p = by_head(jnp.sum(v, axis=0))[:, 0:1] / float(nb * s.n_dev)
    dev = v - mean_p
    squares = by_head(jnp.sum(jnp.where(lane1 < 64, cells * dev * dev, v), axis=0))
    inv_p = lax.rsqrt((squares[:, 0:1] + squares[:, 64:65]) / s.count + epsilon)
    gain_p = jnp.where(iota((8, 1), 0) < nb, r.hng[0], r.hng[1])
    shift_p = jnp.where(iota((8, 1), 0) < nb, r.hns[0], r.hns[1])
    xhat_p = (p8 - mean_p) * inv_p
    feature, back_p = gelu_both(xhat_p * gain_p + shift_p)
    flat = jnp.where(valid, feature, 0.0).astype(bf16)
    one_lane = first_head & (lane == s.side)
    flat_f = flat.astype(f32)
    lhs0 = jnp.where(one_lane, 1.0, jnp.where(first_head, flat_f, 0.0))
    lhs1 = jnp.where(first_head, 0.0, flat_f)
    pad8 = jnp.zeros((8, s.line), f32)

    def tall(v):
        return jnp.concatenate([v, pad8[:, : v.shape[1]]], axis=0).astype(bf16)

    half = (dot(tall(lhs0), r.dk[0]) + dot(tall(lhs1), r.dk[1]))[0:8]
    logits = half + pltpu.roll(half, nb, 0)
    move = iota((8, s.mp), 1)
    r.legal_v[...] = jnp.zeros_like(r.legal_v)
    r.legal_v[0:nb, 0 : s.moves] = r.legal[...]
    r.legal_v[nb : 2 * nb, 0 : s.moves] = r.legal[...]
    masked = jnp.where(r.legal_v[...] == 1, logits, negative_fill)
    top = jnp.max(masked, axis=1, keepdims=True)
    terms = jnp.exp(masked - top)
    total = jnp.sum(terms, axis=1, keepdims=True)
    row_b = iota((8, 1), 0) & (nb - 1)
    target = jnp.where(
        row_b < 2,
        jnp.where(row_b == 0, r.target[0], r.target[1]),
        jnp.where(row_b == 2, r.target[2], r.target[3]),
    )
    chosen = move == target
    picked = jnp.sum(jnp.where(chosen, logits, 0.0), axis=1, keepdims=True)
    ce = top + jnp.log(total) - picked
    dl = (terms / total - chosen.astype(f32)).astype(bf16).astype(f32)
    first_move = iota((8, s.mp), 0) < nb
    dq = dot_nt(tall(jnp.where(first_move, dl, 0.0)), r.dk[0]) + dot_nt(
        tall(jnp.where(first_move, 0.0, dl)), r.dk[1]
    )
    dnh = jnp.where(valid, dq[0:8] * back_p, 0.0)
    gain_row = jnp.sum(dnh * xhat_p, axis=1, keepdims=True)
    shift_row = jnp.sum(dnh, axis=1, keepdims=True)
    r.st4[...] = jnp.where(lane1 < 32, gain_row, jnp.where(lane1 < 64, shift_row, ce))
    x_send(3, r.st4, r.t4)
    r.fd_own[...] = jnp.zeros_like(r.fd_own)
    r.fd_own[0:8, :] = flat_f
    r.fd_own[8:16, 0 : s.mp] = dl
    r.fd_send[...] = r.fd_own[...].astype(bf16)
    x_send(6, r.fd_send, r.fd)
    x_wait(3, r.t4)
    sums = by_head(jnp.sum(r.t4[...], axis=0))
    gain_sum, shift_sum = sums[:, 0:1], sums[:, 32:33]
    r.loss[...] = sums[0:1, 64:65] / float(nb * s.n_dev)
    pair = jnp.where(iota((1, lanes), 1) == 0, sums[0:1, :], sums[4:5, :])
    pair_gain = jnp.where(iota((1, lanes), 1) == 0, sums[0:1, 0:1], sums[4:5, 0:1])
    pair_shift = jnp.where(iota((1, lanes), 1) == 0, sums[0:1, 32:33], sums[4:5, 32:33])
    r.hng_grad[0:1, :] = pair_gain[:, 0:2]
    r.hng_grad[1:2, :] = pair_shift[:, 0:2]
    dp = gain_p * inv_p * (dnh - (shift_sum + xhat_p * gain_sum) / s.count)
    dp = jnp.where(valid, dp, 0.0)
    r.dp_full[0:16, :] = tall(dp)

    spread_p = dot_nt(r.expand[...], r.dp_full[...])
    row, col = iota((s.rows, lanes), 0), iota((s.rows, lanes), 1)
    spread_p = jnp.where((row & (nb - 1)) == (col & (nb - 1)), spread_p, 0.0).astype(bf16)
    r.up[...] = dot(spread_p, r.hc_full[...])

    def sums_back(field, xhat, carry):
        f = field.reshape(br // 8, 8, ch)
        g = (field * xhat).reshape(br // 8, 8, ch)
        return carry[0] + jnp.sum(g, axis=0), carry[1] + jnp.sum(f, axis=0)

    def back2(i, carry):
        at = rows_of(i)
        dz = (r.cot_r[at, :].astype(f32) + r.up[at, :]) * r.dz[at, :]
        dz = jnp.where(inside, dz, 0.0)
        r.dz[at, :] = dz
        return sums_back(dz, (r.h2[at, :] - mean2) * inv2, carry)

    zero = jnp.zeros((8, ch), f32)
    g2, s2 = lax.fori_loop(0, s.side, back2, (zero, zero))
    r.st5[0:1, :] = jnp.sum(g2, axis=0, keepdims=True)
    r.st5[1:2, :] = jnp.sum(s2, axis=0, keepdims=True)
    x_send(4, r.st5, r.t5)

    head_grad = jnp.zeros((16, ch), f32)
    dp_f = r.dp_full[0:16, :].astype(f32)
    for b in range(nb):
        rows_b = jnp.where((iota((16, s.line), 0) & (nb - 1)) == b, dp_f, 0.0).astype(bf16)
        head_grad = head_grad + dot(rows_b, r.outp[b].astype(bf16))
    r.st6[2:3, :] = head_grad[0:1] + head_grad[1:2] + head_grad[2:3] + head_grad[3:4]
    r.st6[3:4, :] = head_grad[4:5] + head_grad[5:6] + head_grad[6:7] + head_grad[7:8]
    x_wait(4, r.t5)
    t5 = jnp.sum(r.t5[...], axis=0)
    g2s, s2s = t5[0:1], t5[1:2]

    def to_field2(i, _):
        at = rows_of(i)
        xhat = (r.h2[at, :] - mean2) * inv2
        d = (gain2 * inv2) * (r.dz[at, :] - (s2s + xhat * g2s) * (1.0 / s.count))
        store3(r.d3, i, jnp.where(inside, d, 0.0))
        return 0

    lax.fori_loop(0, s.side, to_field2, 0)

    def wgrad(planes_t, di):
        start = 2 * br - br * di
        return dot(planes_t[...], r.d3[start : start + s.rows, :])

    for di in range(3):
        rs_fill(di, wgrad(r.at, di), rs2)
        if s.fast:
            rs_cross(rs2, di)
    rs_fill_rest(rs2)
    if not s.fast:
        rs_cross(rs2, 0)
    conv(r.d3, r.wb2, r.h2)
    for part in range(s.nch):
        rs_plane(rs2, part)

    def back1(i, carry):
        at = rows_of(i)
        dn = jnp.where(inside, r.h2[at, :] * r.back1[at, :], 0.0)
        r.h2[at, :] = dn
        return sums_back(dn, (r.h1[at, :] - mean1) * inv1, carry)

    g1, s1 = lax.fori_loop(0, s.side, back1, (zero, zero))
    r.st6[0:1, :] = jnp.sum(g1, axis=0, keepdims=True)
    r.st6[1:2, :] = jnp.sum(s1, axis=0, keepdims=True)
    x_send(5, r.st6, r.t6)
    for part in range(s.nch):
        rs_line(rs2, part)
    x_wait(5, r.t6)
    t6 = jnp.sum(r.t6[...], axis=0)
    g1s, s1s = t6[0:1], t6[1:2]

    def to_field1(i, _):
        at = rows_of(i)
        xhat = (r.h1[at, :] - mean1) * inv1
        d = (gain1 * inv1) * (r.h2[at, :] - (s1s + xhat * g1s) * (1.0 / s.count))
        store3(r.d3, i, jnp.where(inside, d, 0.0))
        return 0

    lax.fori_loop(0, s.side, to_field1, 0)
    for di in range(3):
        rs_fill(di, wgrad(r.xt, di), rs1)
        if s.fast:
            rs_cross(rs1, di)
    rs_fill_rest(rs1)
    if not s.fast:
        rs_cross(rs1, 0)
    for part in range(s.nch):
        rs_plane(rs1, part)
    conv(r.d3, r.wb1, r.h1)
    for part in range(s.nch):
        rs_line(rs1, part)

    def result(i, _):
        at = rows_of(i)
        up = dot(gather_up, (r.dz[at, :] + r.h1[at, :]).astype(bf16))
        for b in range(nb):
            r.in_grad[b, i] = up[gap * b : gap * b + s.side].astype(bf16)
        return 0

    lax.fori_loop(0, s.side, result, 0)
    shares = jnp.concatenate([g1s, g2s, s1s, s2s, t6[2:4], jnp.zeros((2, ch), f32)], axis=0)
    r.share[...] = pltpu.roll(shares, lax.rem(ch - w * me, ch), 1)
    r.gains_grad[...] = r.share[0:2, 0:w]
    r.shifts_grad[...] = r.share[2:4, 0:w]
    r.hc_grad[...] = r.share[4:6, 0:w]

    x_wait(6, r.fd)
    fd = r.fd[...].astype(f32)
    features = fd[:, 0:8, :].reshape(8 * s.n_dev, s.line).astype(bf16)
    dls = fd[:, 8:16, 0 : s.mp].reshape(8 * s.n_dev, s.mp).astype(bf16)
    t = iota((s.rp, 1), 0)
    source = s.rsh * me + t
    mine = (t < s.rsh) & (source < s.head_in)
    col = iota((s.rp, s.line), 1)
    col8 = iota((s.rp, 8 * s.n_dev), 1) & 7
    own = jnp.where((t < s.rsh) & (source == s.head_in) & (col8 < nb), 1.0, 0.0)
    for k in range(2):
        in_k = mine & (source >= k * s.cells) & (source < (k + 1) * s.cells)
        cell = jnp.where(in_k, source - k * s.cells, 0)
        cell_i = divided(cell, s.side, s.cells)
        place = jnp.where(in_k, cell_i * gap + (cell - cell_i * s.side), -1)
        pick = (col == place).astype(f32).astype(bf16)
        rows_k = dot_nt(pick, features)
        own = own + jnp.where((col8 >= nb) if k else (col8 < nb), rows_k, 0.0)
    grad = dot(own.astype(bf16), dls)
    r.dense_v[...] = grad
    r.dense_grad[...] = r.dense_v[0 : s.rsh, 0 : s.moves]

    for part in range(s.nch):
        rs_finish(rs2, part, r.c2_grad)
    for part in range(s.nch):
        rs_finish(rs1, part, r.c1_grad)

    for u in range(len(units)):
        g_drain(u)
    for number, slots in enumerate((r.t1, r.t2, r.t3, r.t4, r.t5, r.t6, r.fd)):
        x_drain(number, slots)
    rs_drain(rs1)
    rs_drain(rs2)


def body(x, w1, w2, gains, shifts, hc, hng, hns, dense, legal, target, cot):
    s = sizes_of(lax.axis_size("gx"), lax.axis_size("gy"), x, w1, dense, legal.shape[1])
    vmem, smem, hbm = pltpu.VMEM, pltpu.SMEM, pl.ANY
    inputs = dict(
        x=(x, hbm), w1=(w1, vmem), w2=(w2, vmem), gains=(gains, vmem), shifts=(shifts, vmem), hc=(hc, vmem),
        hng=(hng, smem), hns=(hns, smem), dense=(dense, vmem), legal=(legal, vmem), target=(target, smem), cot=(cot, hbm),
    )
    outputs = dict(
        out=(x.shape, bf16), loss=((1, 1), f32), in_grad=(x.shape, bf16), c1_grad=(w1.shape, f32),
        c2_grad=(w2.shape, f32), gains_grad=(gains.shape, f32), shifts_grad=(shifts.shape, f32),
        hc_grad=(hc.shape, f32), hng_grad=((2, 2), f32), dense_grad=(dense.shape, f32),
    )
    gxn, qn, n, ch = s.gx_n, s.q_n, s.n_dev, s.ch
    field = pltpu.VMEM((s.rows, ch), f32)
    planes = pltpu.VMEM((s.padded, 3 * ch), bf16)
    turned = pltpu.VMEM((ch, s.rows), bf16)
    weight = pltpu.VMEM((3, 3 * ch, ch), bf16)
    two = pltpu.VMEM((2, ch), f32)
    four = pltpu.VMEM((4, ch), f32)
    tile = pltpu.VMEM((8, lanes), f32)
    dma = pltpu.SemaphoreType.DMA
    scratch = dict(
        local_sem=dma((2,)), g_sem=dma((2 * s.nch + 1, 7)), x_sem=dma((7, 2)),
        rs_sem1=dma((s.nch, 6)), rs_sem2=dma((s.nch, 6)),
        x_v=pltpu.VMEM(x.shape, bf16), cot_v=pltpu.VMEM(x.shape, bf16),
        stage=pltpu.VMEM((s.blk1, lanes), f32), small=pltpu.VMEM((8, lanes), f32),
        s1=pltpu.VMEM((gxn, qn, 2, s.blk1, lanes), bf16), s2=pltpu.VMEM((gxn, qn, 2, s.blk, lanes), bf16),
        sd=pltpu.VMEM((gxn, qn, 2, s.rp, s.mp), bf16), dense_v=pltpu.VMEM((s.rp, s.mp), f32),
        x3=planes, a3=planes, d3=planes, slab=pltpu.VMEM((s.nb * s.gap, ch), f32),
        outp=pltpu.VMEM((s.nb, s.line, ch), f32), cot_r=pltpu.VMEM((s.rows, ch), bf16),
        xt=turned, at=turned, wt1=weight, wt2=weight, wb1=weight, wb2=weight,
        pars=pltpu.VMEM((8, ch), f32), h1=field, h2=field, dz=field, back1=field, up=field,
        st1=two, t1=pltpu.VMEM((n, 2, ch), f32), st2=two, t2=pltpu.VMEM((n, 2, ch), f32),
        st3=tile, t3=pltpu.VMEM((n, 8, lanes), f32), st4=tile, t4=pltpu.VMEM((n, 8, lanes), f32),
        st5=two, t5=pltpu.VMEM((n, 2, ch), f32), st6=four, t6=pltpu.VMEM((n, 4, ch), f32),
        fd_own=pltpu.VMEM((16, s.line), f32), fd_send=pltpu.VMEM((16, s.line), bf16),
        fd=pltpu.VMEM((n, 16, s.line), bf16),
        dk=pltpu.VMEM((2, s.line, s.mp), bf16), expand=pltpu.VMEM((s.rows, s.line), bf16),
        dp_full=pltpu.VMEM((lanes, s.line), bf16), hc_full=pltpu.VMEM((lanes, ch), bf16),
        legal_v=pltpu.VMEM((8, s.mp), jnp.int32), share=pltpu.VMEM((8, ch), f32),
    )
    if not s.fast:
        scratch["flat"] = pltpu.VMEM((9, ch, ch), f32)
        scratch["eight"] = pltpu.VMEM((9, 8, ch), f32)
    for number in ("1", "2"):
        scratch["rsb" + number] = pltpu.VMEM((s.nch, 2, gxn, qn, s.crows, lanes), bf16)
        scratch["rc" + number] = pltpu.VMEM((s.nch, gxn, qn, s.crows, lanes), bf16)
        scratch["pb" + number] = pltpu.VMEM((s.nch, qn, gxn, s.crows, lanes), bf16)
        scratch["rp" + number] = pltpu.VMEM((s.nch, qn - 1, gxn, s.crows, lanes), bf16)
        scratch["zb" + number] = pltpu.VMEM((s.nch, gxn, s.crows, lanes), bf16)
        scratch["rz" + number] = pltpu.VMEM((s.nch, gxn - 1, s.crows, lanes), bf16)
    run = pl.pallas_call(
        functools.partial(kernel, s, tuple(inputs), tuple(outputs), tuple(scratch)),
        out_shape=[jax.ShapeDtypeStruct(shape, kind) for shape, kind in outputs.values()],
        in_specs=[pl.BlockSpec(memory_space=space) for _, space in inputs.values()],
        out_specs=[pl.BlockSpec(memory_space=vmem) for _ in outputs],
        scratch_shapes=list(scratch.values()),
        compiler_params=pltpu.CompilerParams(
            collective_id=0, has_side_effects=True, vmem_limit_bytes=60 * 1024 * 1024
        ),
        cost_estimate=pl.CostEstimate(flops=10_500_000_000, bytes_accessed=8_000_000, transcendentals=800_000),
        name="tower",
    )
    results = run(*(value for value, _ in inputs.values()))
    return (results[0], results[1].reshape(()), *results[2:])


def solution(mesh):
    both = ("gx", "gy")
    board = P(both, None, None, None)
    kernels = P(None, both, None)
    pairs = P(None, both)
    return jax.shard_map(
        body,
        mesh=mesh,
        in_specs=(
            board, kernels, kernels, pairs, pairs, pairs, P(), P(), P(both, None), P(both, None), P(both), board,
        ),
        out_specs=(board, P(), board, kernels, kernels, pairs, pairs, pairs, P(), P(both, None)),
        check_vma=False,
    )
```

time: 930 us -> 119 us (0.13); the launches traced: 920 us -> 118 us
  blocking collectives: 596 us -> 0 us
  waiting for transfers between devices: 131 us -> 0 us
  Pallas kernels: 0 us -> 104 us
  local copies, waits for them, and re-layouts: 68.9 us -> 11.7 us
  matrix products: 52.8 us -> 0 us
  other arithmetic: 32.2 us -> 0 us
  starting transfers between devices: 22.1 us -> 0 us
  between operations: 16.6 us -> 2.39 us
    psum x9 -> x0, blocking collectives: 360 us -> none  [the longest x3 126 us: norm_stats(): lax.psum(jnp.sum(deviation * deviation, axis=over_axes, keepdims=True), (...]
    all_gather x4 -> x0, blocking collectives: 156 us -> none  [the longest x1 45.1 us: body(): lax.all_gather(dense_weight, ('gx', 'gy'), axis=0, tiled=True)]
    reduce_scatter x2 -> x0, waiting for transfers between devices: 130 us -> none  [the longest x1 130 us: body(): lax.psum_scatter(second_term, ('gx', 'gy'), scatter_dimension=1, tiled=True)]
    pallas_call x0 -> x1, Pallas kernels: none -> 104 us  [body(): results = run(*(value for value, _ in inputs.values()))]
    unnamed x1 -> x0, blocking collectives: 79.4 us -> none
    dot_general x24 -> x0, matrix products: 34 us -> none  [the longest x18 24.5 us: kernel_grad(): lax.dot_general(window, grad_rows, (((0,), (0,)), ((), ())), preferred_el...]
    unnamed x9 -> x0, starting transfers between devices: 22 us -> none
    conv_general_dilated x4 -> x0, matrix products: 18.8 us -> none  [convolve(): lax.conv_general_dilated(planes, filters, (1, 1), 'SAME', dimension_numbe...]
  transfers between devices with their start and end apart: 13 -> 0, of which waited for: 1 -> 0; matrix products, arithmetic and copies ran while one was open for 15% -> 0% of each run, Pallas kernels for 0% -> 0%
where the time goes in v1:
time: 119 us; the launch traced here: 118 us
  Pallas kernels  104 us (87%)
  local copies, waits for them, and re-layouts  11.7 us (10%)
  between operations  2.39 us (2%)
    pallas_call x1, Pallas kernels, body(): results = run(*(value for value, _ in inputs.values()))  104 us
    unnamed x29, local copies, waits for them, and re-layouts  11.7 us

profile of v1, /device:TPU:0, one launch (start us, length us, event | category | flops | bytes accessed | tf_op | source)
XLA Modules:
  0.0 118.2 jit_solution(14874217056981142816)
XLA Ops:
  0.6 0.0 copy-start.1
  0.7 2.3 %copy.22.refs_0_ = bf16[4,19,19,256]{3,2,1,0:T(8,128)(2,1)} copy(bf16[4,19,19,256]{3,0,2,1:T(4,128)(2,1)} %param.12) | data formatting | bytes 1478656 | tf_op args[0]
  2.9 0.0 copy-done.1
  2.9 1.1 copy.23.refs_11_
  4.0 104.1 %tower.1 = (bf16[4,19,19,256]{3,2,1,0:T(8,128)(2,1)}, f32[1,1]{1,0:T(1,128)}, bf16[4,19,19,256]{3,2,1,0:T(8,128)(2,1)}, f32[9,8,256]{2,1,0:T(8,128)}, f32[9,8,25...) custom-call(bf16[4,19,19,256]{3,2,1,0:T(8,128)(2,1)} %copy.22.refs_0, ...), custom_call_target="tpu_custom_call" | custom-call | flops 10499999744 | bytes 8000000 | tf_op jit(solution)/shard_map/tower/pallas_call | solution.py:798
  108.2 0.0 copy-start
  108.2 2.4 %copy.24 = bf16[4,19,19,256]{3,0,2,1:T(4,128)(2,1)} copy(bf16[4,19,19,256]{3,2,1,0:T(8,128)(2,1)} %get-tuple-element.30) | data formatting | bytes 1478656
  110.6 0.0 copy-done
  110.6 0.0 copy-start.3
  110.6 1.2 copy.25
  112.3 0.0 copy-done.3
  112.3 0.0 copy-start.2
  112.3 0.6 copy.35
  113.0 0.3 copy-done.2
  113.2 0.0 copy-start.8
  113.2 0.0 copy-start.4
  113.2 0.6 copy.36
  113.9 0.0 copy-done.8
  113.9 0.0 copy-start.7
  113.9 0.6 copy.37
  114.5 0.1 copy-done.7
  114.6 0.0 copy-start.6
  114.6 0.6 copy.38
  115.1 0.1 copy-done.6
  115.3 0.0 copy-start.5
  115.3 0.6 copy.39
  115.8 0.1 copy-done.5
  115.9 0.6 copy.40
  116.4 0.0 copy-done.4
  116.4 0.6 copy.41
Async XLA Ops:
  0.6 2.3 %copy-start.1 = (bf16[4,19,19,256]{3,0,2,1:T(4,128)(2,1)S(1)}, bf16[4,19,19,256]{3,0,2,1:T(4,128)(2,1)}, u32[]{:S(2)}) copy-start(bf16[4,19,19,256]{3,0,2,1:T(4,128)(2,1)} %param.23) | copy-start | bytes 2217988
  108.2 2.4 %copy-start = (bf16[4,19,19,256]{3,2,1,0:T(8,128)(2,1)S(1)}, bf16[4,19,19,256]{3,2,1,0:T(8,128)(2,1)}, u32[]{:S(2)}) copy-start(bf16[4,19,19,256]{3,2,1,0:T(8,128)(2,1)} %get-tuple-element.32) | copy-start | bytes 2217988
  110.6 1.7 %copy-start.3 = (f32[9,8,256]{2,1,0:T(8,128)S(1)}, f32[9,8,256]{2,1,0:T(8,128)}, u32[]{:S(2)}) copy-start(f32[9,8,256]{2,1,0:T(8,128)} %get-tuple-element.53) | copy-start | bytes 221188
  112.3 0.9 copy-start.2
  113.2 0.7 copy-start.8
  113.2 3.2 %copy-start.4 = (f32[23,362]{1,0:T(8,128)S(1)}, f32[23,362]{1,0:T(8,128)}, u32[]{:S(2)}) copy-start(f32[23,362]{1,0:T(8,128)} %get-tuple-element.59) | copy-start | bytes 99916
  113.9 0.7 copy-start.7
  114.6 0.7 copy-start.6
  115.3 0.6 copy-start.5

commit v2 on v1

--- a/solution.py
+++ b/solution.py
@@ -23,10 +23,11 @@
 
 
 def divided(values, divisor, limit):
-    factor = -(-65536 // divisor)
-    for n in range(limit):
-        assert (n * factor) >> 16 == n // divisor and n * factor < 2**31
-    return lax.shift_right_logical(values * factor, jnp.int32(16))
+    for shift in range(16, 24):
+        factor = -(-(1 << shift) // divisor)
+        if all((n * factor) >> shift == n // divisor and n * factor < 2**31 for n in range(limit)):
+            return lax.shift_right_logical(values * factor, jnp.int32(shift))
+    raise ValueError("no factor")
 
 
 def iota(shape, axis):
@@ -41,6 +42,11 @@
     return v * half, back
 
 
+def gelu(v):
+    half = 0.5 * v
+    return half + half * jnp.tanh(v * (root + (root * cube) * (v * v)))
+
+
 def dot(left, right):
     return jnp.dot(left, right, preferred_element_type=f32)
 
@@ -52,14 +58,14 @@
 def sizes_of(gx_n, gy_n, x, w1, dense, moves):
     s = types.SimpleNamespace()
     s.gx_n, s.gy_n, s.q_n, s.n_dev = gx_n, gy_n, gy_n // 2, gx_n * gy_n
-    s.nb, s.side, s.ch = x.shape[0], x.shape[1], x.shape[3]
+    s.side, s.nb, s.ch = x.shape[0], x.shape[2], x.shape[3]
     s.w = w1.shape[1]
     s.wide = s.side + 1
     s.br = s.wide * s.nb
     s.rows = s.side * s.br
     s.padded = s.rows + 2 * s.br
-    s.gap = up_to(s.side, 8)
-    s.line = up_to(s.side * s.gap, lanes)
+    s.line = up_to(s.side * s.wide, lanes)
+    s.long = up_to(s.rows, lanes)
     s.cells = s.side * s.side
     s.moves = moves
     s.mp = up_to(moves, lanes)
@@ -72,7 +78,8 @@
     s.nch = 3 if s.fast else 1
     s.crows = s.blk // s.nch
     s.count = float(s.nb * s.cells * s.n_dev)
-    assert s.nb == 4 and s.br % 16 == 0 and gy_n % 2 == 0 and 8 % s.w == 0
+    assert s.nb == 4 and s.br % 16 == 0 and 8 % s.w == 0
+    assert gx_n & (gx_n - 1) == 0 and gy_n & (gy_n - 1) == 0 and gy_n > 1
     return s
 
 
@@ -82,13 +89,13 @@
     q, c = lax.div(gy, 2), lax.rem(gy, 2)
     me = gx * s.gy_n + gy
     other = (gx, gy + 1 - 2 * c)
-    gxn, qn, nb, br, gap, ch = s.gx_n, s.q_n, s.nb, s.br, s.gap, s.ch
+    gxn, qn, nb, br, wide, ch = s.gx_n, s.q_n, s.nb, s.br, s.wide, s.ch
 
     def z_peer(k):
-        return lax.rem(gx + k, gxn)
+        return gx ^ k
 
     def q_peer(j):
-        return lax.rem(q + j, qn)
+        return q ^ j
 
     def send(src, dst, out_sem, in_sem, device):
         pltpu.make_async_remote_copy(
@@ -104,10 +111,12 @@
     partners += [other]
     for p in partners:
         pl.semaphore_signal(barrier, inc=1, device_id=p, device_id_type=MESH)
-    fetch_x = pltpu.make_async_copy(r.x, r.x_v, r.local_sem.at[0])
+    fetch_x = pltpu.make_async_copy(r.x, r.x_v.at[:, pl.ds(0, s.side)], r.local_sem.at[0])
     fetch_x.start()
-    fetch_cot = pltpu.make_async_copy(r.cot, r.cot_v, r.local_sem.at[1])
+    fetch_cot = pltpu.make_async_copy(r.cot, r.cot_v.at[:, pl.ds(0, s.side)], r.local_sem.at[1])
     fetch_cot.start()
+    for fields in (r.x_v, r.cot_v):
+        fields[:, s.side] = jnp.zeros((s.side, nb, ch), bf16)
 
     w = s.w
 
@@ -134,14 +143,6 @@
     for planes in (r.x3, r.a3, r.d3):
         planes[0:br, :] = jnp.zeros((br, 3 * ch), bf16)
         planes[s.padded - br :, :] = jnp.zeros((br, 3 * ch), bf16)
-    r.slab[...] = jnp.zeros_like(r.slab)
-    r.outp[:, s.side * gap :, :] = jnp.zeros((nb, s.line - s.side * gap, ch), f32)
-    row, col = iota((br, nb * gap), 0), iota((br, nb * gap), 1)
-    j_of, b_of = lax.shift_right_logical(row, 2), row & 3
-    spread = ((col == b_of * gap + j_of) & (j_of < s.side)).astype(f32).astype(bf16)
-    row, col = iota((nb * gap, br), 0), iota((nb * gap, br), 1)
-    j_of, b_of = lax.shift_right_logical(col, 2), col & 3
-    gather_up = ((row == b_of * gap + j_of) & (j_of < s.side)).astype(f32).astype(bf16)
     inside = iota((br, ch), 0) < nb * s.side
 
     def store3(planes, i, block):
@@ -153,17 +154,14 @@
     def rows_of(i):
         return pl.ds(pl.multiple_of(i * br, 16), br)
 
-    def to_rows(source, i):
-        for b in range(nb):
-            r.slab[gap * b : gap * b + s.side, :] = source[b, i].astype(f32)
-        return dot(spread, r.slab[...].astype(bf16))
+    def from_board(block):
+        return block.astype(f32).reshape(br, ch)
+
+    def to_board(block):
+        return block.reshape(wide, nb, ch)[0 : s.side].astype(bf16)
 
     def x_rows(i, _):
-        store3(r.x3, i, to_rows(r.x_v, i))
-        return 0
-
-    def cot_rows(i, _):
-        r.cot_r[rows_of(i), :] = to_rows(r.cot_v, i).astype(bf16)
+        store3(r.x3, i, from_board(r.x_v[i]))
         return 0
 
     fetch_x.wait()
@@ -173,48 +171,48 @@
 
     def span(unit):
         store, part = unit
-        if store is r.sd:
-            return pl.ds(0, s.rp)
+        if store is r.sd or store is r.fd:
+            return pl.ds(0, store.shape[3])
         whole = s.blk1 if store is r.s1 else s.blk
         if s.nch == 1:
             return pl.ds(0, whole)
         start = part * s.crows
         return pl.ds(start, whole - start if part == s.nch - 1 else s.crows)
 
-    units = [(r.s1, p) for p in range(s.nch)] + [(r.s2, p) for p in range(s.nch)] + [(r.sd, 0)]
+    units = [(r.s1, p) for p in range(s.nch)] + [(r.s2, p) for p in range(s.nch)] + [(r.sd, 0), (r.fd, 0)]
 
     def g_start(u):
         store, at = units[u][0], span(units[u])
         own = store.at[gx, q, c, at]
-        for k in range(gxn - 1, 0, -1):
-            send(own, own, r.g_sem.at[u, 0], r.g_sem.at[u, 1], (z_peer(k), gy))
-        for j in range(1, qn):
-            send(own, own, r.g_sem.at[u, 2], r.g_sem.at[u, 3], (gx, 2 * q_peer(j) + c))
+        for k in range(1, gxn):
+            send(own, own, r.g_sem.at[u, 0], r.g_sem.at[u, 5 + k], (z_peer(k), gy))
+        for j in range(qn - 1, 0, -1):
+            send(own, own, r.g_sem.at[u, 1], r.g_sem.at[u, 4], (gx, 2 * q_peer(j) + c))
 
     def g_forward(u):
         store, at = units[u][0], span(units[u])
-        take(r.g_sem.at[u, 1], store.at[pl.ds(0, gxn - 1), 0, 0, at])
         for k in range(1, gxn):
             block = store.at[z_peer(k), q, c, at]
-            for j in range(1, qn):
-                send(block, block, r.g_sem.at[u, 4], r.g_sem.at[u, 3], (gx, 2 * q_peer(j) + c))
+            take(r.g_sem.at[u, 5 + k], block)
+            for j in range(qn - 1, 0, -1):
+                send(block, block, r.g_sem.at[u, 2], r.g_sem.at[u, 4], (gx, 2 * q_peer(j) + c))
 
     def g_cross(u):
         store, at = units[u][0], span(units[u])
-        take(r.g_sem.at[u, 3], store.at[:, pl.ds(0, qn - 1), 0, at])
+        take(r.g_sem.at[u, 4], store.at[:, pl.ds(0, qn - 1), 0, at])
         block = store.at[:, :, c, at]
-        send(block, block, r.g_sem.at[u, 5], r.g_sem.at[u, 6], other)
+        send(block, block, r.g_sem.at[u, 3], r.g_sem.at[u, 5], other)
 
     def g_done(u):
         store, at = units[u][0], span(units[u])
-        take(r.g_sem.at[u, 6], store.at[:, :, 0, at])
+        take(r.g_sem.at[u, 5], store.at[:, :, 0, at])
 
     def g_drain(u):
         store, at = units[u][0], span(units[u])
         take(r.g_sem.at[u, 0], store.at[pl.ds(0, gxn - 1), 0, 0, at])
-        take(r.g_sem.at[u, 2], store.at[0, pl.ds(0, qn - 1), 0, at])
-        take(r.g_sem.at[u, 4], store.at[pl.ds(0, gxn - 1), pl.ds(0, qn - 1), 0, at])
-        take(r.g_sem.at[u, 5], store.at[:, :, 0, at])
+        take(r.g_sem.at[u, 1], store.at[0, pl.ds(0, qn - 1), 0, at])
+        take(r.g_sem.at[u, 2], store.at[pl.ds(0, gxn - 1), pl.ds(0, qn - 1), 0, at])
+        take(r.g_sem.at[u, 3], store.at[:, :, 0, at])
 
     def shard_of(store, d):
         return store[lax.div(d, s.gy_n), lax.div(lax.rem(d, s.gy_n), 2), lax.rem(d, 2)]
@@ -261,13 +259,19 @@
         r.pars[...] = jnp.transpose(rows)[0:8, :]
 
     def x_send(number, src, slots):
-        def one(n, _):
-            k = s.n_dev - 1 - n
-            device = (lax.rem(gx + lax.div(k, s.gy_n), gxn), lax.rem(gy + lax.rem(k, s.gy_n), s.gy_n))
+        def one(k):
+            device = (gx ^ lax.div(k, s.gy_n), gy ^ lax.rem(k, s.gy_n))
             send(src, slots.at[me], r.x_sem.at[number, 0], r.x_sem.at[number, 1], device)
-            return 0
-
-        lax.fori_loop(0, s.n_dev - 1, one, 0)
+
+        if s.n_dev <= 64:
+            hops = {k: k // s.gy_n + bin(k % s.gy_n // 2).count("1") for k in range(1, s.n_dev)}
+            for k in sorted(hops, key=lambda k: (-hops[k], k)):
+                send(
+                    src, slots.at[me], r.x_sem.at[number, 0], r.x_sem.at[number, 1],
+                    (gx ^ (k // s.gy_n), gy ^ (k % s.gy_n)),
+                )
+        else:
+            lax.fori_loop(0, s.n_dev - 1, lambda n, _: (one(s.n_dev - 1 - n), 0)[1], 0)
         slots[me] = src[...]
 
     def x_wait(number, slots):
@@ -383,15 +387,11 @@
         g_start(u)
     for u in range(n1):
         g_forward(u)
-    for u in range(n1, len(units)):
+    for u in range(n1, 2 * n1):
         g_start(u)
-    fetch_cot.wait()
-    lax.fori_loop(0, s.side, cot_rows, 0)
     r.xt[...] = jnp.transpose(r.x3[br : br + s.rows, ch : 2 * ch])
     for u in range(n1):
         g_cross(u)
-    for u in range(n1, 2 * n1):
-        g_forward(u)
 
     def conv_part(planes, weight, di, out):
         v = dot(planes[br * di : br * di + s.rows, :], weight[di])
@@ -412,10 +412,10 @@
     local_stats(r.h1, r.st1)
     x_send(0, r.st1, r.t1)
 
+    for u in range(n1, 2 * n1):
+        g_forward(u)
+    g_start(2 * n1)
     unpack_small()
-    for u in range(n1, 2 * n1):
-        g_cross(u)
-    g_forward(2 * n1)
 
     def flip(weight, back):
         for di in range(3):
@@ -423,37 +423,46 @@
                 tap = weight[2 - di, (2 - dj) * ch : (3 - dj) * ch, :]
                 back[di, dj * ch : (dj + 1) * ch, :] = jnp.transpose(tap)
 
-    flip(r.wt1, r.wb1)
+    for u in range(n1, 2 * n1):
+        g_cross(u)
+    g_forward(2 * n1)
+
+    gain1, gain2 = r.pars[0:1, :], r.pars[1:2, :]
+    shift1, shift2 = r.pars[2:3, :], r.pars[3:4, :]
+    hc0, hc1 = r.pars[4:5, :], r.pars[5:6, :]
+
+    x_wait(0, r.t1)
+    mean1, inv1 = global_stats(r.t1)
+
+    def act1(i, _):
+        n = (r.h1[rows_of(i), :] - mean1) * (inv1 * gain1) + shift1
+        a = gelu(n)
+        store3(r.a3, i, jnp.where(inside, a, 0.0))
+        return 0
+
+    lax.fori_loop(0, s.side, act1, 0)
     for u in range(n1, 2 * n1):
         g_done(u)
         unpack(r.s2, u - n1, r.wt2)
-
-    gain1, gain2 = r.pars[0:1, :], r.pars[1:2, :]
-    shift1, shift2 = r.pars[2:3, :], r.pars[3:4, :]
-    hc0, hc1 = r.pars[4:5, :], r.pars[5:6, :]
-
-    x_wait(0, r.t1)
-    mean1, inv1 = global_stats(r.t1)
-
-    def act1(i, _):
-        n = (r.h1[rows_of(i), :] - mean1) * (inv1 * gain1) + shift1
-        a, back = gelu_both(n)
-        r.back1[rows_of(i), :] = back
-        store3(r.a3, i, jnp.where(inside, a, 0.0))
-        return 0
-
-    lax.fori_loop(0, s.side, act1, 0)
     conv(r.a3, r.wt2, r.h2)
     local_stats(r.h2, r.st2)
     x_send(1, r.st2, r.t2)
 
     r.at[...] = jnp.transpose(r.a3[br : br + s.rows, ch : 2 * ch])
+    flip(r.wt1, r.wb1)
     flip(r.wt2, r.wb2)
+
+    def slope1(i, _):
+        n = (r.h1[rows_of(i), :] - mean1) * (inv1 * gain1) + shift1
+        r.back1[rows_of(i), :] = gelu_both(n)[1]
+        return 0
+
+    lax.fori_loop(0, s.side, slope1, 0)
     g_cross(2 * n1)
     g_done(2 * n1)
     at = iota((s.line, 1), 0)
-    i_of = divided(at, gap, s.line)
-    j_of = at - i_of * gap
+    i_of = divided(at, wide, s.line)
+    j_of = at - i_of * wide
     used = (i_of < s.side) & (j_of < s.side)
     wide_slots = s.n_dev * s.rp
     shard_rows = iota((s.line, wide_slots), 1)
@@ -470,16 +479,16 @@
         place = jnp.where(wanted, shard * s.rp + (source - shard * s.rsh), -1)
         pick = (shard_rows == place).astype(f32).astype(bf16)
         r.dk[k] = dot(pick, dense_all).astype(bf16)
-    row, col = iota((s.rows, s.line), 0), iota((s.rows, s.line), 1)
-    row_line = lax.shift_right_logical(iota((s.rows, 1), 0), 2)
-    row_i = divided(row_line, s.wide, s.rows // nb)
-    row_at = row_i * gap + (row_line - row_i * s.wide)
-    r.expand[...] = (col == row_at).astype(f32).astype(bf16)
+    row, col = iota((s.long, s.line), 0), iota((s.long, s.line), 1)
+    r.expand[...] = (col == lax.shift_right_logical(row, 2)).astype(f32).astype(bf16)
+    r.out_r[s.rows :, :] = jnp.zeros((s.long - s.rows, ch), bf16)
     r.dp_full[...] = jnp.zeros_like(r.dp_full)
     r.hc_full[...] = jnp.zeros_like(r.hc_full)
     row = iota((16, ch), 0)
     both = jnp.where(row < nb, hc0, jnp.where(row < 2 * nb, hc1, 0.0))
     r.hc_full[0:16, :] = both.astype(bf16)
+    hc_rows = jnp.where(row == 0, hc0, jnp.where(row == 1, hc1, 0.0)).astype(bf16)
+    fetch_cot.wait()
 
     x_wait(1, r.t2)
     mean2, inv2 = global_stats(r.t2)
@@ -488,26 +497,19 @@
         at = rows_of(i)
         xin = r.x3[pl.ds(pl.multiple_of((i + 1) * br, 16), br), ch : 2 * ch].astype(f32)
         z = xin + ((r.h2[at, :] - mean2) * (inv2 * gain2) + shift2)
-        a, back = gelu_both(z)
-        r.dz[at, :] = back
-        up = dot(gather_up, jnp.where(inside, a, 0.0).astype(bf16))
-        for b in range(nb):
-            r.outp[b, pl.ds(pl.multiple_of(i * gap, 8), gap), :] = up[gap * b : gap * b + gap]
-            r.out[b, i] = up[gap * b : gap * b + s.side].astype(bf16)
+        r.dz[at, :] = z
+        a = jnp.where(inside, gelu(z), 0.0)
+        r.out_r[at, :] = a.astype(bf16)
+        r.out_v[i] = to_board(a)
         return 0
 
     lax.fori_loop(0, s.side, act2, 0)
-    row = iota((8, s.line), 0)
-    lane = iota((8, s.line), 1)
-    lane_i = divided(lane, gap, s.line)
-    valid = (lane_i < s.side) & (lane - lane_i * gap < s.side)
-    first_head = row < nb
-    row256 = iota((16, ch), 0)
-    p8 = jnp.zeros((8, s.line), f32)
-    for b in range(nb):
-        head = jnp.where(row256 == b, hc0, jnp.where(row256 == nb + b, hc1, 0.0)).astype(bf16)
-        p8 = p8 + dot_nt(head, r.outp[b].astype(bf16))[0:8]
-
+    put_out = pltpu.make_async_copy(r.out_v, r.out, r.local_sem.at[2])
+    put_out.start()
+    p_long = dot_nt(hc_rows, r.out_r[...])[0:8]
+    lane = iota((8, s.long), 1)
+    lane_j = lane - divided(lane, br, s.long) * br
+    valid_long = (lane_j < nb * s.side) & (lane < s.rows)
     row1, lane1 = iota((8, lanes), 0), iota((8, lanes), 1)
 
     def by_head(v):
@@ -515,18 +517,49 @@
         b = v[4:5] + v[5:6] + v[6:7] + v[7:8]
         return jnp.where(iota(v.shape, 0) < nb, a, b)
 
-    cells = float(s.cells)
-    mean_row = jnp.sum(jnp.where(valid, p8, 0.0), axis=1, keepdims=True) / cells
-    dev = jnp.where(valid, p8 - mean_row, 0.0)
+    n_local = float(nb * s.cells)
+    mean_row = jnp.sum(jnp.where(valid_long, p_long, 0.0), axis=1, keepdims=True) / n_local
+    dev = jnp.where(valid_long, p_long - mean_row, 0.0)
     square_row = jnp.sum(dev * dev, axis=1, keepdims=True)
-    r.st3[...] = jnp.where(lane1 < 64, mean_row, square_row)
+    lane3 = iota((1, lanes), 1)
+    means = jnp.where(lane3 < 32, mean_row[0:1], mean_row[1:2])
+    r.st3[...] = jnp.where(lane3 < 64, means, jnp.where(lane3 < 96, square_row[0:1], square_row[1:2]))
     x_send(2, r.st3, r.t3)
+
+    def slope2(i, _):
+        r.dz[rows_of(i), :] = gelu_both(r.dz[rows_of(i), :])[1]
+        return 0
+
+    lax.fori_loop(0, s.side, slope2, 0)
+    row = iota((8, s.long), 0)
+    wanted = (lane & (nb - 1)) == (row & (nb - 1))
+    rest = jnp.where(wanted, jnp.where(row < nb, p_long[0:1], p_long[1:2]), 0.0)
+    parts = []
+    for _ in range(3):
+        part = rest.astype(bf16).astype(f32)
+        parts.append(part)
+        rest = rest - part
+    parts = jnp.concatenate(parts + [jnp.zeros_like(rest)], axis=0).astype(bf16)
+    p8 = dot(parts, r.expand[...])
+    p8 = p8[0:8] + p8[8:16] + p8[16:24]
+    row = iota((8, s.line), 0)
+    lane = iota((8, s.line), 1)
+    lane_i = divided(lane, wide, s.line)
+    valid = (lane_i < s.side) & (lane - lane_i * wide < s.side)
+    first_head = row < nb
+
     x_wait(2, r.t3)
     v = r.t3[...]
-    mean_p = by_head(jnp.sum(v, axis=0))[:, 0:1] / float(nb * s.n_dev)
-    dev = v - mean_p
-    squares = by_head(jnp.sum(jnp.where(lane1 < 64, cells * dev * dev, v), axis=0))
-    inv_p = lax.rsqrt((squares[:, 0:1] + squares[:, 64:65]) / s.count + epsilon)
+    mean_k = jnp.sum(v, axis=0) / float(s.n_dev)
+    dev = v - mean_k
+    squares = jnp.sum(jnp.where(lane3 < 64, n_local * dev * dev, v), axis=0)
+
+    def of_head(v, at):
+        return jnp.where(iota((8, 1), 0) < nb, v[:, at : at + 1], v[:, at + 32 : at + 33])
+
+    mean_p = of_head(mean_k, 0)
+    squares = of_head(squares, 0) + of_head(squares, 64)
+    inv_p = lax.rsqrt(squares / s.count + epsilon)
     gain_p = jnp.where(iota((8, 1), 0) < nb, r.hng[0], r.hng[1])
     shift_p = jnp.where(iota((8, 1), 0) < nb, r.hns[0], r.hns[1])
     xhat_p = (p8 - mean_p) * inv_p
@@ -573,8 +606,8 @@
     r.fd_own[...] = jnp.zeros_like(r.fd_own)
     r.fd_own[0:8, :] = flat_f
     r.fd_own[8:16, 0 : s.mp] = dl
-    r.fd_send[...] = r.fd_own[...].astype(bf16)
-    x_send(6, r.fd_send, r.fd)
+    r.fd[gx, q, c] = r.fd_own[...].astype(bf16)
+    g_start(2 * n1 + 1)
     x_wait(3, r.t4)
     sums = by_head(jnp.sum(r.t4[...], axis=0))
     gain_sum, shift_sum = sums[:, 0:1], sums[:, 32:33]
@@ -588,9 +621,10 @@
     dp = jnp.where(valid, dp, 0.0)
     r.dp_full[0:16, :] = tall(dp)
 
-    spread_p = dot_nt(r.expand[...], r.dp_full[...])
+    spread_p = dot_nt(r.expand[0 : s.rows, :], r.dp_full[...])
     row, col = iota((s.rows, lanes), 0), iota((s.rows, lanes), 1)
     spread_p = jnp.where((row & (nb - 1)) == (col & (nb - 1)), spread_p, 0.0).astype(bf16)
+    r.spread[...] = spread_p
     r.up[...] = dot(spread_p, r.hc_full[...])
 
     def sums_back(field, xhat, carry):
@@ -600,7 +634,7 @@
 
     def back2(i, carry):
         at = rows_of(i)
-        dz = (r.cot_r[at, :].astype(f32) + r.up[at, :]) * r.dz[at, :]
+        dz = (from_board(r.cot_v[i]) + r.up[at, :]) * r.dz[at, :]
         dz = jnp.where(inside, dz, 0.0)
         r.dz[at, :] = dz
         return sums_back(dz, (r.h2[at, :] - mean2) * inv2, carry)
@@ -610,12 +644,11 @@
     r.st5[0:1, :] = jnp.sum(g2, axis=0, keepdims=True)
     r.st5[1:2, :] = jnp.sum(s2, axis=0, keepdims=True)
     x_send(4, r.st5, r.t5)
-
-    head_grad = jnp.zeros((16, ch), f32)
-    dp_f = r.dp_full[0:16, :].astype(f32)
-    for b in range(nb):
-        rows_b = jnp.where((iota((16, s.line), 0) & (nb - 1)) == b, dp_f, 0.0).astype(bf16)
-        head_grad = head_grad + dot(rows_b, r.outp[b].astype(bf16))
+    g_forward(2 * n1 + 1)
+
+    head_grad = lax.dot_general(
+        r.spread[...], r.out_r[0 : s.rows, :], (((0,), (0,)), ((), ())), preferred_element_type=f32
+    )
     r.st6[2:3, :] = head_grad[0:1] + head_grad[1:2] + head_grad[2:3] + head_grad[3:4]
     r.st6[3:4, :] = head_grad[4:5] + head_grad[5:6] + head_grad[6:7] + head_grad[7:8]
     x_wait(4, r.t5)
@@ -635,6 +668,19 @@
         start = 2 * br - br * di
         return dot(planes_t[...], r.d3[start : start + s.rows, :])
 
+    conv(r.d3, r.wb2, r.h2)
+    g_cross(2 * n1 + 1)
+
+    def back1(i, carry):
+        at = rows_of(i)
+        dn = jnp.where(inside, r.h2[at, :] * r.back1[at, :], 0.0)
+        r.h2[at, :] = dn
+        return sums_back(dn, (r.h1[at, :] - mean1) * inv1, carry)
+
+    g1, s1 = lax.fori_loop(0, s.side, back1, (zero, zero))
+    r.st6[0:1, :] = jnp.sum(g1, axis=0, keepdims=True)
+    r.st6[1:2, :] = jnp.sum(s1, axis=0, keepdims=True)
+    x_send(5, r.st6, r.t6)
     for di in range(3):
         rs_fill(di, wgrad(r.at, di), rs2)
         if s.fast:
@@ -642,22 +688,8 @@
     rs_fill_rest(rs2)
     if not s.fast:
         rs_cross(rs2, 0)
-    conv(r.d3, r.wb2, r.h2)
     for part in range(s.nch):
         rs_plane(rs2, part)
-
-    def back1(i, carry):
-        at = rows_of(i)
-        dn = jnp.where(inside, r.h2[at, :] * r.back1[at, :], 0.0)
-        r.h2[at, :] = dn
-        return sums_back(dn, (r.h1[at, :] - mean1) * inv1, carry)
-
-    g1, s1 = lax.fori_loop(0, s.side, back1, (zero, zero))
-    r.st6[0:1, :] = jnp.sum(g1, axis=0, keepdims=True)
-    r.st6[1:2, :] = jnp.sum(s1, axis=0, keepdims=True)
-    x_send(5, r.st6, r.t6)
-    for part in range(s.nch):
-        rs_line(rs2, part)
     x_wait(5, r.t6)
     t6 = jnp.sum(r.t6[...], axis=0)
     g1s, s1s = t6[0:1], t6[1:2]
@@ -678,6 +710,8 @@
     if not s.fast:
         rs_cross(rs1, 0)
     for part in range(s.nch):
+        rs_line(rs2, part)
+    for part in range(s.nch):
         rs_plane(rs1, part)
     conv(r.d3, r.wb1, r.h1)
     for part in range(s.nch):
@@ -685,20 +719,20 @@
 
     def result(i, _):
         at = rows_of(i)
-        up = dot(gather_up, (r.dz[at, :] + r.h1[at, :]).astype(bf16))
-        for b in range(nb):
-            r.in_grad[b, i] = up[gap * b : gap * b + s.side].astype(bf16)
+        r.in_grad_v[i] = to_board(r.dz[at, :] + r.h1[at, :])
         return 0
 
     lax.fori_loop(0, s.side, result, 0)
+    put_in_grad = pltpu.make_async_copy(r.in_grad_v, r.in_grad, r.local_sem.at[3])
+    put_in_grad.start()
     shares = jnp.concatenate([g1s, g2s, s1s, s2s, t6[2:4], jnp.zeros((2, ch), f32)], axis=0)
     r.share[...] = pltpu.roll(shares, lax.rem(ch - w * me, ch), 1)
     r.gains_grad[...] = r.share[0:2, 0:w]
     r.shifts_grad[...] = r.share[2:4, 0:w]
     r.hc_grad[...] = r.share[4:6, 0:w]
 
-    x_wait(6, r.fd)
-    fd = r.fd[...].astype(f32)
+    g_done(2 * n1 + 1)
+    fd = r.fd[...].astype(f32).reshape(s.n_dev, 16, s.line)
     features = fd[:, 0:8, :].reshape(8 * s.n_dev, s.line).astype(bf16)
     dls = fd[:, 8:16, 0 : s.mp].reshape(8 * s.n_dev, s.mp).astype(bf16)
     t = iota((s.rp, 1), 0)
@@ -711,7 +745,7 @@
         in_k = mine & (source >= k * s.cells) & (source < (k + 1) * s.cells)
         cell = jnp.where(in_k, source - k * s.cells, 0)
         cell_i = divided(cell, s.side, s.cells)
-        place = jnp.where(in_k, cell_i * gap + (cell - cell_i * s.side), -1)
+        place = jnp.where(in_k, cell_i * wide + (cell - cell_i * s.side), -1)
         pick = (col == place).astype(f32).astype(bf16)
         rows_k = dot_nt(pick, features)
         own = own + jnp.where((col8 >= nb) if k else (col8 < nb), rows_k, 0.0)
@@ -726,13 +760,29 @@
 
     for u in range(len(units)):
         g_drain(u)
-    for number, slots in enumerate((r.t1, r.t2, r.t3, r.t4, r.t5, r.t6, r.fd)):
+    for number, slots in enumerate((r.t1, r.t2, r.t3, r.t4, r.t5, r.t6)):
         x_drain(number, slots)
     rs_drain(rs1)
     rs_drain(rs2)
+    put_out.wait()
+    put_in_grad.wait()
+
+
+def place(n, *refs):
+    sources, targets, held, (came, went) = refs[:n], refs[n : 2 * n], refs[2 * n : 3 * n], refs[3 * n :]
+    fetch = [pltpu.make_async_copy(sources[i], held[i], came.at[i]) for i in range(n)]
+    put = [pltpu.make_async_copy(held[i], targets[i], went.at[i]) for i in range(n)]
+    for copy in fetch:
+        copy.start()
+    for i in range(n):
+        fetch[i].wait()
+        put[i].start()
+    for copy in put:
+        copy.wait()
 
 
 def body(x, w1, w2, gains, shifts, hc, hng, hns, dense, legal, target, cot):
+    x, cot = (jnp.transpose(v, (1, 2, 0, 3)) for v in (x, cot))
     s = sizes_of(lax.axis_size("gx"), lax.axis_size("gy"), x, w1, dense, legal.shape[1])
     vmem, smem, hbm = pltpu.VMEM, pltpu.SMEM, pl.ANY
     inputs = dict(
@@ -746,6 +796,7 @@
     )
     gxn, qn, n, ch = s.gx_n, s.q_n, s.n_dev, s.ch
     field = pltpu.VMEM((s.rows, ch), f32)
+    boards = pltpu.VMEM((s.side, s.wide, s.nb, ch), bf16)
     planes = pltpu.VMEM((s.padded, 3 * ch), bf16)
     turned = pltpu.VMEM((ch, s.rows), bf16)
     weight = pltpu.VMEM((3, 3 * ch, ch), bf16)
@@ -754,22 +805,20 @@
     tile = pltpu.VMEM((8, lanes), f32)
     dma = pltpu.SemaphoreType.DMA
     scratch = dict(
-        local_sem=dma((2,)), g_sem=dma((2 * s.nch + 1, 7)), x_sem=dma((7, 2)),
+        local_sem=dma((4,)), g_sem=dma((2 * s.nch + 2, 5 + gxn)), x_sem=dma((6, 2)),
         rs_sem1=dma((s.nch, 6)), rs_sem2=dma((s.nch, 6)),
-        x_v=pltpu.VMEM(x.shape, bf16), cot_v=pltpu.VMEM(x.shape, bf16),
+        x_v=boards, cot_v=boards, out_v=pltpu.VMEM(x.shape, bf16), in_grad_v=pltpu.VMEM(x.shape, bf16),
         stage=pltpu.VMEM((s.blk1, lanes), f32), small=pltpu.VMEM((8, lanes), f32),
         s1=pltpu.VMEM((gxn, qn, 2, s.blk1, lanes), bf16), s2=pltpu.VMEM((gxn, qn, 2, s.blk, lanes), bf16),
         sd=pltpu.VMEM((gxn, qn, 2, s.rp, s.mp), bf16), dense_v=pltpu.VMEM((s.rp, s.mp), f32),
-        x3=planes, a3=planes, d3=planes, slab=pltpu.VMEM((s.nb * s.gap, ch), f32),
-        outp=pltpu.VMEM((s.nb, s.line, ch), f32), cot_r=pltpu.VMEM((s.rows, ch), bf16),
+        x3=planes, a3=planes, d3=planes, out_r=pltpu.VMEM((s.long, ch), bf16), spread=pltpu.VMEM((s.rows, lanes), bf16),
         xt=turned, at=turned, wt1=weight, wt2=weight, wb1=weight, wb2=weight,
         pars=pltpu.VMEM((8, ch), f32), h1=field, h2=field, dz=field, back1=field, up=field,
         st1=two, t1=pltpu.VMEM((n, 2, ch), f32), st2=two, t2=pltpu.VMEM((n, 2, ch), f32),
-        st3=tile, t3=pltpu.VMEM((n, 8, lanes), f32), st4=tile, t4=pltpu.VMEM((n, 8, lanes), f32),
+        st3=pltpu.VMEM((1, lanes), f32), t3=pltpu.VMEM((n, 1, lanes), f32), st4=tile, t4=pltpu.VMEM((n, 8, lanes), f32),
         st5=two, t5=pltpu.VMEM((n, 2, ch), f32), st6=four, t6=pltpu.VMEM((n, 4, ch), f32),
-        fd_own=pltpu.VMEM((16, s.line), f32), fd_send=pltpu.VMEM((16, s.line), bf16),
-        fd=pltpu.VMEM((n, 16, s.line), bf16),
-        dk=pltpu.VMEM((2, s.line, s.mp), bf16), expand=pltpu.VMEM((s.rows, s.line), bf16),
+        fd_own=pltpu.VMEM((16, s.line), f32), fd=pltpu.VMEM((gxn, qn, 2, 16, s.line), bf16),
+        dk=pltpu.VMEM((2, s.line, s.mp), bf16), expand=pltpu.VMEM((s.long, s.line), bf16),
         dp_full=pltpu.VMEM((lanes, s.line), bf16), hc_full=pltpu.VMEM((lanes, ch), bf16),
         legal_v=pltpu.VMEM((8, s.mp), jnp.int32), share=pltpu.VMEM((8, ch), f32),
     )
@@ -787,7 +836,7 @@
         functools.partial(kernel, s, tuple(inputs), tuple(outputs), tuple(scratch)),
         out_shape=[jax.ShapeDtypeStruct(shape, kind) for shape, kind in outputs.values()],
         in_specs=[pl.BlockSpec(memory_space=space) for _, space in inputs.values()],
-        out_specs=[pl.BlockSpec(memory_space=vmem) for _ in outputs],
+        out_specs=[pl.BlockSpec(memory_space=hbm if n in ("out", "in_grad") else vmem) for n in outputs],
         scratch_shapes=list(scratch.values()),
         compiler_params=pltpu.CompilerParams(
             collective_id=0, has_side_effects=True, vmem_limit_bytes=60 * 1024 * 1024
@@ -796,7 +845,17 @@
         name="tower",
     )
     results = run(*(value for value, _ in inputs.values()))
-    return (results[0], results[1].reshape(()), *results[2:])
+    results = pl.pallas_call(
+        functools.partial(place, len(results)),
+        out_shape=[jax.ShapeDtypeStruct(v.shape, v.dtype) for v in results],
+        in_specs=[pl.BlockSpec(memory_space=hbm) for _ in results],
+        out_specs=[pl.BlockSpec(memory_space=hbm) for _ in results],
+        scratch_shapes=[pltpu.VMEM(v.shape, v.dtype) for v in results] + [dma((len(results),))] * 2,
+        name="place",
+    )(*results)
+    out, loss, in_grad, *rest = results
+    out, in_grad = (jnp.transpose(v, (2, 0, 1, 3)) for v in (out, in_grad))
+    return (out, loss.reshape(()), in_grad, *rest)
 
 
 def solution(mesh):

time: 119 us -> 91.1 us (0.77)
  Pallas kernels: 104 us -> 90.1 us
  local copies, waits for them, and re-layouts: 11.7 us -> 0 us
  between operations: 2.39 us -> 0.82 us
    pallas_call x1, Pallas kernels: 104 us -> 87 us  [body(): results = run(*(value for value, _ in inputs.values()))]
    unnamed x29 -> x0, local copies, waits for them, and re-layouts: 11.7 us -> none
    pallas_call x0 -> x1, Pallas kernels: none -> 3.04 us  [body(): pl.pallas_call(functools.partial(place, len(results)), out_shape=[jax.Sha...]
where the time goes in v2:
time: 91.1 us; the launch traced here: 90.9 us
  Pallas kernels  90.1 us (99%)
    pallas_call x1, Pallas kernels, body(): results = run(*(value for value, _ in inputs.values()))  87 us
    pallas_call x1, Pallas kernels, body(): pl.pallas_call(functools.partial(place, len(results)), out_shape=[jax.Sha...  3.04 us

profile of v2, /device:TPU:0, one launch (start us, length us, event | category | flops | bytes accessed | tf_op | source)
XLA Modules:
  0.0 90.9 jit_solution(16434251542737446177)
XLA Ops:
  0.6 87.0 %tower.1 = (bf16[19,19,4,256]{3,2,1,0:T(4,128)(2,1)}, f32[1,1]{1,0:T(1,128)}, bf16[19,19,4,256]{3,2,1,0:T(4,128)(2,1)}, f32[9,8,256]{2,1,0:T(8,128)}, f32[9,8,25...) custom-call(bf16[19,19,4,256]{3,2,1,0:T(4,128)(2,1)} %bitcast.5, ...), custom_call_target="tpu_custom_call" | custom-call | flops 10499999744 | bytes 8000000 | tf_op jit(solution)/shard_map/tower/pallas_call | solution.py:847
  87.7 3.0 %place.1 = (bf16[19,19,4,256]{3,2,1,0:T(4,128)(2,1)}, f32[1,1]{1,0:T(1,128)}, bf16[19,19,4,256]{3,2,1,0:T(4,128)(2,1)}, f32[9,8,256]{2,1,0:T(8,128)}, f32[9,8,25...) custom-call(bf16[19,19,4,256]{3,2,1,0:T(4,128)(2,1)} %get-tuple-elem, ...), custom_call_target="tpu_custom_call" | custom-call | tf_op jit(solution)/shard_map/place/pallas_call | solution.py:848

commit v3 on v2

--- a/solution.py
+++ b/solution.py
@@ -111,34 +111,40 @@
     partners += [other]
     for p in partners:
         pl.semaphore_signal(barrier, inc=1, device_id=p, device_id_type=MESH)
-    fetch_x = pltpu.make_async_copy(r.x, r.x_v.at[:, pl.ds(0, s.side)], r.local_sem.at[0])
-    fetch_x.start()
-    fetch_cot = pltpu.make_async_copy(r.cot, r.cot_v.at[:, pl.ds(0, s.side)], r.local_sem.at[1])
-    fetch_cot.start()
+    names = ("x", "w1", "w2", "gains", "shifts", "hc", "dense", "cot", "legal", "hng", "hns", "target")
+    fetch = {}
+    for n, name in enumerate(names):
+        held = getattr(r, name + "_v")
+        held = held.at[:, pl.ds(0, s.side)] if name in ("x", "cot") else held
+        fetch[name] = pltpu.make_async_copy(getattr(r, name), held, r.local_sem.at[n])
+        fetch[name].start()
     for fields in (r.x_v, r.cot_v):
         fields[:, s.side] = jnp.zeros((s.side, nb, ch), bf16)
 
     w = s.w
 
-    def stage(weight, rows):
+    def stage(weight):
         r.stage[...] = jnp.zeros_like(r.stage)
         for t in range(9):
             v = weight[t].astype(f32)
             r.stage[2 * w * t : 2 * w * t + w, :] = v[:, :lanes]
             r.stage[2 * w * t + w : 2 * w * t + 2 * w, :] = v[:, lanes:]
 
-    r.small[...] = jnp.zeros_like(r.small)
-    r.small[0:2, 0:w] = r.gains[...].astype(f32)
-    r.small[2:4, 0:w] = r.shifts[...].astype(f32)
-    r.small[4:6, 0:w] = r.hc[...].astype(f32)
-    stage(r.w1, s.blk1)
-    r.stage[18 * w : 19 * w, 0:8] = jnp.transpose(r.small[...])[0:w, :]
-    r.s1[gx, q, c] = r.stage[...].astype(bf16)
-    stage(r.w2, s.blk)
-    r.s2[gx, q, c] = r.stage[0 : s.blk, :].astype(bf16)
-    r.dense_v[...] = jnp.zeros_like(r.dense_v)
-    r.dense_v[0 : s.rsh, 0 : s.moves] = r.dense[...].astype(f32)
-    r.sd[gx, q, c] = r.dense_v[...].astype(bf16)
+    def stage_all():
+        for name in names[1:7]:
+            fetch[name].wait()
+        r.small[...] = jnp.zeros_like(r.small)
+        r.small[0:2, 0:w] = r.gains_v[...].astype(f32)
+        r.small[2:4, 0:w] = r.shifts_v[...].astype(f32)
+        r.small[4:6, 0:w] = r.hc_v[...].astype(f32)
+        stage(r.w1_v)
+        r.stage[18 * w : 19 * w, 0:8] = jnp.transpose(r.small[...])[0:w, :]
+        r.s1[gx, q, c] = r.stage[...].astype(bf16)
+        stage(r.w2_v)
+        r.s2[gx, q, c] = r.stage[0 : s.blk, :].astype(bf16)
+        r.dense_f[...] = jnp.zeros_like(r.dense_f)
+        r.dense_f[0 : s.rsh, 0 : s.moves] = r.dense_v[...].astype(f32)
+        r.sd[gx, q, c] = r.dense_f[...].astype(bf16)
 
     for planes in (r.x3, r.a3, r.d3):
         planes[0:br, :] = jnp.zeros((br, 3 * ch), bf16)
@@ -164,8 +170,9 @@
         store3(r.x3, i, from_board(r.x_v[i]))
         return 0
 
-    fetch_x.wait()
+    fetch["x"].wait()
     lax.fori_loop(0, s.side, x_rows, 0)
+    stage_all()
 
     pl.semaphore_wait(barrier, len(partners))
 
@@ -279,6 +286,19 @@
 
     def x_drain(number, slots):
         take(r.x_sem.at[number, 0], slots.at[pl.ds(0, s.n_dev - 1)])
+
+    def plane_send(number, src, slots):
+        for k in range(s.gy_n - 1, 0, -1):
+            send(src, slots.at[gy], r.x_sem.at[number, 0], r.x_sem.at[number, 1], (gx, gy ^ k))
+        slots[gy] = src[...]
+
+    def line_send(number, src, slots):
+        for k in range(gxn - 1, 0, -1):
+            send(src, slots.at[gx], r.x_sem.at[number, 0], r.x_sem.at[number, 1], (gx ^ k, gy))
+        slots[gx] = src[...]
+
+    def group_wait(number, slots, way=1):
+        take(r.x_sem.at[number, way], slots.at[pl.ds(0, slots.shape[0] - 1)])
 
     def rs_fill(part, grad, b):
         if s.fast:
@@ -321,11 +341,21 @@
         for p in range(qn):
             total = b.rsb[part, c, :, p].astype(f32) + b.rc[part, :, p].astype(f32)
             b.pb[part, p] = total.astype(bf16)
+        if s.nch > 1 and part == s.nch - 1:
+            for k in range(gxn - 1, -1, -1):
+                for j in range(qn - 1, -1, -1):
+                    if k + j:
+                        block = b.pb.at[part, q_peer(j), z_peer(k)]
+                        device = (z_peer(k), 2 * q_peer(j) + c)
+                        send(block, b.rd.at[k * qn + j - 1], b.sem.at[part, 2], b.sem.at[part, 3], device)
+            return
         for j in range(1, qn):
             to = q_peer(j)
             send(b.pb.at[part, to], b.rp.at[part, j - 1], b.sem.at[part, 2], b.sem.at[part, 3], (gx, 2 * to + c))
 
     def rs_line(b, part):
+        if s.nch > 1 and part == s.nch - 1:
+            return
         take(b.sem.at[part, 3], b.rp.at[part])
         total = b.pb[part, q].astype(f32)
         for j in range(qn - 1):
@@ -336,10 +366,14 @@
             send(b.zb.at[part, to], b.rz.at[part, k - 1], b.sem.at[part, 4], b.sem.at[part, 5], (to, gy))
 
     def rs_finish(b, part, out):
-        take(b.sem.at[part, 5], b.rz.at[part])
-        total = b.zb[part, gx].astype(f32)
-        for k in range(gxn - 1):
-            total = total + b.rz[part, k].astype(f32)
+        if s.nch > 1 and part == s.nch - 1:
+            take(b.sem.at[part, 3], b.rd)
+            total = b.pb[part, q, gx].astype(f32) + jnp.sum(b.rd[...].astype(f32), axis=0)
+        else:
+            take(b.sem.at[part, 5], b.rz.at[part])
+            total = b.zb[part, gx].astype(f32)
+            for k in range(gxn - 1):
+                total = total + b.rz[part, k].astype(f32)
         taps = 9 // s.nch
         for t in range(taps):
             at = 2 * w * t
@@ -348,11 +382,14 @@
     def rs_drain(b):
         for part in range(s.nch):
             take(b.sem.at[part, 0], b.rc.at[part])
+            if s.nch > 1 and part == s.nch - 1:
+                take(b.sem.at[part, 2], b.rd)
+                continue
             take(b.sem.at[part, 2], b.rp.at[part])
             take(b.sem.at[part, 4], b.rz.at[part])
 
     def rs_buffers(number):
-        names = ("rsb", "rc", "pb", "rp", "zb", "rz")
+        names = ("rsb", "rc", "pb", "rp", "zb", "rz", "rd")
         b = types.SimpleNamespace(**{n: getattr(r, n + number) for n in names})
         b.sem = getattr(r, "rs_sem" + number)
         return b
@@ -385,10 +422,16 @@
     n1 = s.nch
     for u in range(n1):
         g_start(u)
-    for u in range(n1):
-        g_forward(u)
+    g_forward(0)
     for u in range(n1, 2 * n1):
         g_start(u)
+    for u in range(1, 2 * n1):
+        g_forward(u)
+    g_start(2 * n1)
+    row, col = iota((s.long, s.line), 0), iota((s.long, s.line), 1)
+    r.expand[...] = (col == lax.shift_right_logical(row, 2)).astype(f32).astype(bf16)
+    r.out_r[s.rows :, :] = jnp.zeros((s.long - s.rows, ch), bf16)
+    r.vu[s.rows :, :] = jnp.zeros((s.long - s.rows, 2 * ch), bf16)
     r.xt[...] = jnp.transpose(r.x3[br : br + s.rows, ch : 2 * ch])
     for u in range(n1):
         g_cross(u)
@@ -412,10 +455,9 @@
     local_stats(r.h1, r.st1)
     x_send(0, r.st1, r.t1)
 
-    for u in range(n1, 2 * n1):
-        g_forward(u)
-    g_start(2 * n1)
+    g_forward(2 * n1)
     unpack_small()
+    fetch["cot"].wait()
 
     def flip(weight, back):
         for di in range(3):
@@ -425,7 +467,7 @@
 
     for u in range(n1, 2 * n1):
         g_cross(u)
-    g_forward(2 * n1)
+    flip(r.wt1, r.wb1)
 
     gain1, gain2 = r.pars[0:1, :], r.pars[1:2, :]
     shift1, shift2 = r.pars[2:3, :], r.pars[3:4, :]
@@ -449,8 +491,6 @@
     x_send(1, r.st2, r.t2)
 
     r.at[...] = jnp.transpose(r.a3[br : br + s.rows, ch : 2 * ch])
-    flip(r.wt1, r.wb1)
-    flip(r.wt2, r.wb2)
 
     def slope1(i, _):
         n = (r.h1[rows_of(i), :] - mean1) * (inv1 * gain1) + shift1
@@ -479,16 +519,12 @@
         place = jnp.where(wanted, shard * s.rp + (source - shard * s.rsh), -1)
         pick = (shard_rows == place).astype(f32).astype(bf16)
         r.dk[k] = dot(pick, dense_all).astype(bf16)
-    row, col = iota((s.long, s.line), 0), iota((s.long, s.line), 1)
-    r.expand[...] = (col == lax.shift_right_logical(row, 2)).astype(f32).astype(bf16)
-    r.out_r[s.rows :, :] = jnp.zeros((s.long - s.rows, ch), bf16)
     r.dp_full[...] = jnp.zeros_like(r.dp_full)
     r.hc_full[...] = jnp.zeros_like(r.hc_full)
     row = iota((16, ch), 0)
     both = jnp.where(row < nb, hc0, jnp.where(row < 2 * nb, hc1, 0.0))
     r.hc_full[0:16, :] = both.astype(bf16)
     hc_rows = jnp.where(row == 0, hc0, jnp.where(row == 1, hc1, 0.0)).astype(bf16)
-    fetch_cot.wait()
 
     x_wait(1, r.t2)
     mean2, inv2 = global_stats(r.t2)
@@ -504,7 +540,7 @@
         return 0
 
     lax.fori_loop(0, s.side, act2, 0)
-    put_out = pltpu.make_async_copy(r.out_v, r.out, r.local_sem.at[2])
+    put_out = pltpu.make_async_copy(r.out_v, r.out, r.local_sem.at[len(names)])
     put_out.start()
     p_long = dot_nt(hc_rows, r.out_r[...])[0:8]
     lane = iota((8, s.long), 1)
@@ -526,11 +562,41 @@
     r.st3[...] = jnp.where(lane3 < 64, means, jnp.where(lane3 < 96, square_row[0:1], square_row[1:2]))
     x_send(2, r.st3, r.t3)
 
-    def slope2(i, _):
-        r.dz[rows_of(i), :] = gelu_both(r.dz[rows_of(i), :])[1]
-        return 0
-
-    lax.fori_loop(0, s.side, slope2, 0)
+    for name in names[8:]:
+        fetch[name].wait()
+    r.legal_both[...] = jnp.zeros_like(r.legal_both)
+    r.legal_both[0:nb, 0 : s.moves] = r.legal_v[...]
+    r.legal_both[nb : 2 * nb, 0 : s.moves] = r.legal_v[...]
+
+    def slope2(i, carry):
+        at = rows_of(i)
+        slope = jnp.where(inside, gelu_both(r.dz[at, :])[1], 0.0)
+        r.dz[at, :] = slope
+        scaled = slope * ((r.h2[at, :] - mean2) * inv2)
+        r.vu[at, 0:ch] = slope.astype(bf16)
+        r.vu[at, ch:] = scaled.astype(bf16)
+        cot = from_board(r.cot_v[i])
+        a = (cot * scaled).reshape(br // 8, 8, ch)
+        b = (cot * slope).reshape(br // 8, 8, ch)
+        return carry[0] + jnp.sum(a, axis=0), carry[1] + jnp.sum(b, axis=0)
+
+    zero = jnp.zeros((8, ch), f32)
+    cot_g, cot_s = lax.fori_loop(0, s.side, slope2, (zero, zero))
+    cot_g, cot_s = jnp.sum(cot_g, axis=0, keepdims=True), jnp.sum(cot_s, axis=0, keepdims=True)
+    row = iota((16, s.long), 0)
+    centred = jnp.where(valid_long[0:1], p_long[0:2] - mean_row[0:2], 0.0)
+    against = jnp.where(
+        row == 0, jnp.where(valid_long[0:1], 1.0, 0.0), jnp.where(row == 1, centred[0:1], jnp.where(row == 2, centred[1:2], 0.0))
+    ).astype(bf16)
+    early = dot(against, r.vu[...])
+    for half in range(2):
+        part = early[:, half * ch : (half + 1) * ch]
+        ones = part[0:1]
+        r.ste[4 * half : 4 * half + 1, :] = ones
+        r.ste[4 * half + 1 : 4 * half + 2, :] = part[1:2] + mean_row[0:1] * ones
+        r.ste[4 * half + 2 : 4 * half + 3, :] = part[2:3] + mean_row[1:2] * ones
+        r.ste[4 * half + 3 : 4 * half + 4, :] = jnp.zeros((1, ch), f32)
+    plane_send(3, r.ste, r.te)
     row = iota((8, s.long), 0)
     wanted = (lane & (nb - 1)) == (row & (nb - 1))
     rest = jnp.where(wanted, jnp.where(row < nb, p_long[0:1], p_long[1:2]), 0.0)
@@ -560,8 +626,8 @@
     mean_p = of_head(mean_k, 0)
     squares = of_head(squares, 0) + of_head(squares, 64)
     inv_p = lax.rsqrt(squares / s.count + epsilon)
-    gain_p = jnp.where(iota((8, 1), 0) < nb, r.hng[0], r.hng[1])
-    shift_p = jnp.where(iota((8, 1), 0) < nb, r.hns[0], r.hns[1])
+    gain_p = jnp.where(iota((8, 1), 0) < nb, r.hng_v[0], r.hng_v[1])
+    shift_p = jnp.where(iota((8, 1), 0) < nb, r.hns_v[0], r.hns_v[1])
     xhat_p = (p8 - mean_p) * inv_p
     feature, back_p = gelu_both(xhat_p * gain_p + shift_p)
     flat = jnp.where(valid, feature, 0.0).astype(bf16)
@@ -577,18 +643,15 @@
     half = (dot(tall(lhs0), r.dk[0]) + dot(tall(lhs1), r.dk[1]))[0:8]
     logits = half + pltpu.roll(half, nb, 0)
     move = iota((8, s.mp), 1)
-    r.legal_v[...] = jnp.zeros_like(r.legal_v)
-    r.legal_v[0:nb, 0 : s.moves] = r.legal[...]
-    r.legal_v[nb : 2 * nb, 0 : s.moves] = r.legal[...]
-    masked = jnp.where(r.legal_v[...] == 1, logits, negative_fill)
+    masked = jnp.where(r.legal_both[...] == 1, logits, negative_fill)
     top = jnp.max(masked, axis=1, keepdims=True)
     terms = jnp.exp(masked - top)
     total = jnp.sum(terms, axis=1, keepdims=True)
     row_b = iota((8, 1), 0) & (nb - 1)
     target = jnp.where(
         row_b < 2,
-        jnp.where(row_b == 0, r.target[0], r.target[1]),
-        jnp.where(row_b == 2, r.target[2], r.target[3]),
+        jnp.where(row_b == 0, r.target_v[0], r.target_v[1]),
+        jnp.where(row_b == 2, r.target_v[2], r.target_v[3]),
     )
     chosen = move == target
     picked = jnp.sum(jnp.where(chosen, logits, 0.0), axis=1, keepdims=True)
@@ -601,23 +664,55 @@
     dnh = jnp.where(valid, dq[0:8] * back_p, 0.0)
     gain_row = jnp.sum(dnh * xhat_p, axis=1, keepdims=True)
     shift_row = jnp.sum(dnh, axis=1, keepdims=True)
-    r.st4[...] = jnp.where(lane1 < 32, gain_row, jnp.where(lane1 < 64, shift_row, ce))
-    x_send(3, r.st4, r.t4)
+    scale_p = gain_p * inv_p
+    long_row, long_lane = iota((8, s.long), 0), iota((8, s.long), 1)
+    dnh_long = dot_nt(tall(dnh), r.expand[...])[0:8]
+    dnh_long = jnp.where((long_lane & (nb - 1)) == (long_row & (nb - 1)), dnh_long, 0.0)
+    late = dot(jnp.concatenate([dnh_long, jnp.zeros_like(dnh_long)], axis=0).astype(bf16), r.vu[...])[0:8]
+    head_rows = jnp.where(iota((8, ch), 0) < nb, hc0, hc1) * scale_p
+    late_s = jnp.sum(late[:, 0:ch] * head_rows, axis=0, keepdims=True)
+    late_g = jnp.sum(late[:, ch:] * head_rows, axis=0, keepdims=True)
+    r.st5[0:1, :] = cot_g + late_g
+    r.st5[1:2, :] = cot_s + late_s
+
+    def heads(v):
+        return v[0:1] + v[1:2] + v[2:3] + v[3:4], v[4:5] + v[5:6] + v[6:7] + v[7:8]
+
+    gain_heads, shift_heads, ce_sum = heads(gain_row), heads(shift_row), heads(ce)[0]
+    lane5 = iota((1, ch), 1)
+    low = jnp.where(lane5 < 32, gain_heads[0], gain_heads[1])
+    high = jnp.where(lane5 < 96, shift_heads[0], shift_heads[1])
+    r.st5[2:3, :] = jnp.where(lane5 < 64, low, jnp.where(lane5 < 128, high, ce_sum))
+    x_send(4, r.st5, r.t5)
+    group_wait(3, r.te)
+    r.stl[...] = jnp.sum(r.te[...], axis=0)
+    line_send(7, r.stl, r.tl)
     r.fd_own[...] = jnp.zeros_like(r.fd_own)
     r.fd_own[0:8, :] = flat_f
     r.fd_own[8:16, 0 : s.mp] = dl
     r.fd[gx, q, c] = r.fd_own[...].astype(bf16)
     g_start(2 * n1 + 1)
-    x_wait(3, r.t4)
-    sums = by_head(jnp.sum(r.t4[...], axis=0))
-    gain_sum, shift_sum = sums[:, 0:1], sums[:, 32:33]
-    r.loss[...] = sums[0:1, 64:65] / float(nb * s.n_dev)
-    pair = jnp.where(iota((1, lanes), 1) == 0, sums[0:1, :], sums[4:5, :])
-    pair_gain = jnp.where(iota((1, lanes), 1) == 0, sums[0:1, 0:1], sums[4:5, 0:1])
-    pair_shift = jnp.where(iota((1, lanes), 1) == 0, sums[0:1, 32:33], sums[4:5, 32:33])
-    r.hng_grad[0:1, :] = pair_gain[:, 0:2]
-    r.hng_grad[1:2, :] = pair_shift[:, 0:2]
-    dp = gain_p * inv_p * (dnh - (shift_sum + xhat_p * gain_sum) / s.count)
+    flip(r.wt2, r.wb2)
+    x_wait(4, r.t5)
+    group_wait(7, r.tl)
+    te = jnp.sum(r.tl[...], axis=0)
+    t5 = jnp.sum(r.t5[...], axis=0)
+    sums = t5[2:3]
+    gain_sums, shift_sums = (sums[:, 0:1], sums[:, 32:33]), (sums[:, 64:65], sums[:, 96:97])
+    r.tiny[0:1, :] = jnp.broadcast_to(sums[:, 128:129] / float(nb * s.n_dev), (1, lanes))
+    first_lane = iota((1, lanes), 1) == 0
+    r.tiny[1:2, :] = jnp.where(first_lane, *gain_sums)
+    r.tiny[2:3, :] = jnp.where(first_lane, *shift_sums)
+    gain_sum = jnp.where(iota((8, 1), 0) < nb, *gain_sums)
+    shift_sum = jnp.where(iota((8, 1), 0) < nb, *shift_sums)
+    g2s, s2s = t5[0:1], t5[1:2]
+    for k in range(2):
+        weight = (hc0, hc1)[k] * (scale_p[nb * k : nb * k + 1] / s.count)
+        gain_part = gain_sums[k] * inv_p[nb * k : nb * k + 1]
+        mean_k = mean_p[nb * k : nb * k + 1]
+        s2s = s2s - weight * (shift_sums[k] * te[0:1] + gain_part * (te[k + 1 : k + 2] - mean_k * te[0:1]))
+        g2s = g2s - weight * (shift_sums[k] * te[4:5] + gain_part * (te[k + 5 : k + 6] - mean_k * te[4:5]))
+    dp = scale_p * (dnh - (shift_sum + xhat_p * gain_sum) / s.count)
     dp = jnp.where(valid, dp, 0.0)
     r.dp_full[0:16, :] = tall(dp)
 
@@ -632,33 +727,12 @@
         g = (field * xhat).reshape(br // 8, 8, ch)
         return carry[0] + jnp.sum(g, axis=0), carry[1] + jnp.sum(f, axis=0)
 
-    def back2(i, carry):
-        at = rows_of(i)
-        dz = (from_board(r.cot_v[i]) + r.up[at, :]) * r.dz[at, :]
-        dz = jnp.where(inside, dz, 0.0)
-        r.dz[at, :] = dz
-        return sums_back(dz, (r.h2[at, :] - mean2) * inv2, carry)
-
-    zero = jnp.zeros((8, ch), f32)
-    g2, s2 = lax.fori_loop(0, s.side, back2, (zero, zero))
-    r.st5[0:1, :] = jnp.sum(g2, axis=0, keepdims=True)
-    r.st5[1:2, :] = jnp.sum(s2, axis=0, keepdims=True)
-    x_send(4, r.st5, r.t5)
-    g_forward(2 * n1 + 1)
-
-    head_grad = lax.dot_general(
-        r.spread[...], r.out_r[0 : s.rows, :], (((0,), (0,)), ((), ())), preferred_element_type=f32
-    )
-    r.st6[2:3, :] = head_grad[0:1] + head_grad[1:2] + head_grad[2:3] + head_grad[3:4]
-    r.st6[3:4, :] = head_grad[4:5] + head_grad[5:6] + head_grad[6:7] + head_grad[7:8]
-    x_wait(4, r.t5)
-    t5 = jnp.sum(r.t5[...], axis=0)
-    g2s, s2s = t5[0:1], t5[1:2]
-
     def to_field2(i, _):
         at = rows_of(i)
         xhat = (r.h2[at, :] - mean2) * inv2
-        d = (gain2 * inv2) * (r.dz[at, :] - (s2s + xhat * g2s) * (1.0 / s.count))
+        dz = (from_board(r.cot_v[i]) + r.up[at, :]) * r.dz[at, :]
+        r.dz[at, :] = dz
+        d = (gain2 * inv2) * (dz - (s2s + xhat * g2s) * (1.0 / s.count))
         store3(r.d3, i, jnp.where(inside, d, 0.0))
         return 0
 
@@ -668,8 +742,12 @@
         start = 2 * br - br * di
         return dot(planes_t[...], r.d3[start : start + s.rows, :])
 
+    early = 1 if s.fast else 0
+    for di in range(early):
+        rs_fill(di, wgrad(r.at, di), rs2)
+        rs_cross(rs2, di)
+    g_forward(2 * n1 + 1)
     conv(r.d3, r.wb2, r.h2)
-    g_cross(2 * n1 + 1)
 
     def back1(i, carry):
         at = rows_of(i)
@@ -681,15 +759,24 @@
     r.st6[0:1, :] = jnp.sum(g1, axis=0, keepdims=True)
     r.st6[1:2, :] = jnp.sum(s1, axis=0, keepdims=True)
     x_send(5, r.st6, r.t6)
-    for di in range(3):
+    head_grad = lax.dot_general(
+        r.spread[...], r.out_r[0 : s.rows, :], (((0,), (0,)), ((), ())), preferred_element_type=f32
+    )
+    r.sth[0:1, :] = head_grad[0:1] + head_grad[1:2] + head_grad[2:3] + head_grad[3:4]
+    r.sth[1:2, :] = head_grad[4:5] + head_grad[5:6] + head_grad[6:7] + head_grad[7:8]
+    x_send(6, r.sth, r.th)
+    for part in range(early):
+        rs_plane(rs2, part)
+    for di in range(early, 3):
         rs_fill(di, wgrad(r.at, di), rs2)
         if s.fast:
             rs_cross(rs2, di)
     rs_fill_rest(rs2)
     if not s.fast:
         rs_cross(rs2, 0)
-    for part in range(s.nch):
+    for part in range(early, s.nch - 1):
         rs_plane(rs2, part)
+    g_cross(2 * n1 + 1)
     x_wait(5, r.t6)
     t6 = jnp.sum(r.t6[...], axis=0)
     g1s, s1s = t6[0:1], t6[1:2]
@@ -701,21 +788,21 @@
         store3(r.d3, i, jnp.where(inside, d, 0.0))
         return 0
 
+    rs_plane(rs2, s.nch - 1)
     lax.fori_loop(0, s.side, to_field1, 0)
     for di in range(3):
         rs_fill(di, wgrad(r.xt, di), rs1)
         if s.fast:
             rs_cross(rs1, di)
+            if di:
+                rs_plane(rs1, di - 1)
     rs_fill_rest(rs1)
     if not s.fast:
         rs_cross(rs1, 0)
+    rs_plane(rs1, s.nch - 1)
+    conv(r.d3, r.wb1, r.h1)
     for part in range(s.nch):
         rs_line(rs2, part)
-    for part in range(s.nch):
-        rs_plane(rs1, part)
-    conv(r.d3, r.wb1, r.h1)
-    for part in range(s.nch):
-        rs_line(rs1, part)
 
     def result(i, _):
         at = rows_of(i)
@@ -723,13 +810,14 @@
         return 0
 
     lax.fori_loop(0, s.side, result, 0)
-    put_in_grad = pltpu.make_async_copy(r.in_grad_v, r.in_grad, r.local_sem.at[3])
+    put_in_grad = pltpu.make_async_copy(r.in_grad_v, r.in_grad, r.local_sem.at[len(names) + 1])
     put_in_grad.start()
-    shares = jnp.concatenate([g1s, g2s, s1s, s2s, t6[2:4], jnp.zeros((2, ch), f32)], axis=0)
-    r.share[...] = pltpu.roll(shares, lax.rem(ch - w * me, ch), 1)
-    r.gains_grad[...] = r.share[0:2, 0:w]
-    r.shifts_grad[...] = r.share[2:4, 0:w]
-    r.hc_grad[...] = r.share[4:6, 0:w]
+    x_wait(6, r.th)
+    shares = jnp.concatenate([g1s, g2s, s1s, s2s, jnp.sum(r.th[...], axis=0), jnp.zeros((2, ch), f32)], axis=0)
+    r.tiny[8:16, :] = pltpu.roll(shares, lax.rem(ch - w * me, ch), 1)[:, 0:lanes]
+
+    for part in range(s.nch):
+        rs_line(rs1, part)
 
     g_done(2 * n1 + 1)
     fd = r.fd[...].astype(f32).reshape(s.n_dev, 16, s.line)
@@ -750,8 +838,7 @@
         rows_k = dot_nt(pick, features)
         own = own + jnp.where((col8 >= nb) if k else (col8 < nb), rows_k, 0.0)
     grad = dot(own.astype(bf16), dls)
-    r.dense_v[...] = grad
-    r.dense_grad[...] = r.dense_v[0 : s.rsh, 0 : s.moves]
+    r.dense_grad[...] = grad
 
     for part in range(s.nch):
         rs_finish(rs2, part, r.c2_grad)
@@ -760,23 +847,39 @@
 
     for u in range(len(units)):
         g_drain(u)
-    for number, slots in enumerate((r.t1, r.t2, r.t3, r.t4, r.t5, r.t6)):
-        x_drain(number, slots)
+    for number, slots in enumerate((r.t1, r.t2, r.t3, None, r.t5, r.t6, r.th)):
+        if number != 3:
+            x_drain(number, slots)
+    group_wait(3, r.te, 0)
+    group_wait(7, r.tl, 0)
     rs_drain(rs1)
     rs_drain(rs2)
     put_out.wait()
     put_in_grad.wait()
 
 
-def place(n, *refs):
-    sources, targets, held, (came, went) = refs[:n], refs[n : 2 * n], refs[2 * n : 3 * n], refs[3 * n :]
-    fetch = [pltpu.make_async_copy(sources[i], held[i], came.at[i]) for i in range(n)]
-    put = [pltpu.make_async_copy(held[i], targets[i], went.at[i]) for i in range(n)]
+def place(w, x_ref, in_x_ref, c1, c2, dense, tiny, *refs):
+    (out, loss, in_grad, c1_out, c2_out, gains, shifts, hc, hng, dense_out), refs = refs[:10], refs[10:]
+    (out_v, in_v, c1_v, c2_v, dense_v, tiny_v), (came, went) = refs[:6], refs[6:]
+    sources, held = (tiny, dense, c1, c2, x_ref, in_x_ref), (tiny_v, dense_v, c1_v, c2_v, out_v, in_v)
+    fetch = [pltpu.make_async_copy(a, b, came.at[i]) for i, (a, b) in enumerate(zip(sources, held))]
+    put = [
+        pltpu.make_async_copy(a, b, went.at[i])
+        for i, (a, b) in enumerate(((c1_v, c1_out), (c2_v, c2_out), (out_v, out), (in_v, in_grad)))
+    ]
     for copy in fetch:
         copy.start()
-    for i in range(n):
-        fetch[i].wait()
+    for i in range(4):
+        fetch[i + 2].wait()
         put[i].start()
+    fetch[0].wait()
+    fetch[1].wait()
+    loss[...] = tiny_v[0:1, 0:1]
+    hng[...] = tiny_v[1:3, 0:2]
+    gains[...] = tiny_v[8:10, 0:w]
+    shifts[...] = tiny_v[10:12, 0:w]
+    hc[...] = tiny_v[12:14, 0:w]
+    dense_out[...] = dense_v[0 : dense_out.shape[0], 0 : dense_out.shape[1]]
     for copy in put:
         copy.wait()
 
@@ -784,15 +887,14 @@
 def body(x, w1, w2, gains, shifts, hc, hng, hns, dense, legal, target, cot):
     x, cot = (jnp.transpose(v, (1, 2, 0, 3)) for v in (x, cot))
     s = sizes_of(lax.axis_size("gx"), lax.axis_size("gy"), x, w1, dense, legal.shape[1])
-    vmem, smem, hbm = pltpu.VMEM, pltpu.SMEM, pl.ANY
+    vmem, hbm = pltpu.VMEM, pl.ANY
     inputs = dict(
-        x=(x, hbm), w1=(w1, vmem), w2=(w2, vmem), gains=(gains, vmem), shifts=(shifts, vmem), hc=(hc, vmem),
-        hng=(hng, smem), hns=(hns, smem), dense=(dense, vmem), legal=(legal, vmem), target=(target, smem), cot=(cot, hbm),
+        x=x, w1=w1, w2=w2, gains=gains, shifts=shifts, hc=hc, hng=hng, hns=hns, dense=dense, legal=legal,
+        target=target, cot=cot,
     )
     outputs = dict(
-        out=(x.shape, bf16), loss=((1, 1), f32), in_grad=(x.shape, bf16), c1_grad=(w1.shape, f32),
-        c2_grad=(w2.shape, f32), gains_grad=(gains.shape, f32), shifts_grad=(shifts.shape, f32),
-        hc_grad=(hc.shape, f32), hng_grad=((2, 2), f32), dense_grad=(dense.shape, f32),
+        out=(x.shape, bf16), in_grad=(x.shape, bf16), c1_grad=(w1.shape, f32), c2_grad=(w2.shape, f32),
+        dense_grad=((s.rp, s.mp), f32), tiny=((16, lanes), f32),
     )
     gxn, qn, n, ch = s.gx_n, s.q_n, s.n_dev, s.ch
     field = pltpu.VMEM((s.rows, ch), f32)
@@ -801,27 +903,31 @@
     turned = pltpu.VMEM((ch, s.rows), bf16)
     weight = pltpu.VMEM((3, 3 * ch, ch), bf16)
     two = pltpu.VMEM((2, ch), f32)
-    four = pltpu.VMEM((4, ch), f32)
-    tile = pltpu.VMEM((8, lanes), f32)
+    eight = pltpu.VMEM((8, ch), f32)
     dma = pltpu.SemaphoreType.DMA
     scratch = dict(
-        local_sem=dma((4,)), g_sem=dma((2 * s.nch + 2, 5 + gxn)), x_sem=dma((6, 2)),
+        local_sem=dma((14,)), g_sem=dma((2 * s.nch + 2, 5 + gxn)), x_sem=dma((8, 2)),
         rs_sem1=dma((s.nch, 6)), rs_sem2=dma((s.nch, 6)),
         x_v=boards, cot_v=boards, out_v=pltpu.VMEM(x.shape, bf16), in_grad_v=pltpu.VMEM(x.shape, bf16),
         stage=pltpu.VMEM((s.blk1, lanes), f32), small=pltpu.VMEM((8, lanes), f32),
         s1=pltpu.VMEM((gxn, qn, 2, s.blk1, lanes), bf16), s2=pltpu.VMEM((gxn, qn, 2, s.blk, lanes), bf16),
-        sd=pltpu.VMEM((gxn, qn, 2, s.rp, s.mp), bf16), dense_v=pltpu.VMEM((s.rp, s.mp), f32),
+        sd=pltpu.VMEM((gxn, qn, 2, s.rp, s.mp), bf16), dense_f=pltpu.VMEM((s.rp, s.mp), f32),
         x3=planes, a3=planes, d3=planes, out_r=pltpu.VMEM((s.long, ch), bf16), spread=pltpu.VMEM((s.rows, lanes), bf16),
         xt=turned, at=turned, wt1=weight, wt2=weight, wb1=weight, wb2=weight,
         pars=pltpu.VMEM((8, ch), f32), h1=field, h2=field, dz=field, back1=field, up=field,
         st1=two, t1=pltpu.VMEM((n, 2, ch), f32), st2=two, t2=pltpu.VMEM((n, 2, ch), f32),
-        st3=pltpu.VMEM((1, lanes), f32), t3=pltpu.VMEM((n, 1, lanes), f32), st4=tile, t4=pltpu.VMEM((n, 8, lanes), f32),
-        st5=two, t5=pltpu.VMEM((n, 2, ch), f32), st6=four, t6=pltpu.VMEM((n, 4, ch), f32),
+        st3=pltpu.VMEM((1, lanes), f32), t3=pltpu.VMEM((n, 1, lanes), f32), ste=eight, te=pltpu.VMEM((s.gy_n, 8, ch), f32), stl=eight, tl=pltpu.VMEM((gxn, 8, ch), f32),
+        st5=pltpu.VMEM((3, ch), f32), t5=pltpu.VMEM((n, 3, ch), f32), st6=two, t6=pltpu.VMEM((n, 2, ch), f32),
+        sth=two, th=pltpu.VMEM((n, 2, ch), f32), vu=pltpu.VMEM((s.long, 2 * ch), bf16),
         fd_own=pltpu.VMEM((16, s.line), f32), fd=pltpu.VMEM((gxn, qn, 2, 16, s.line), bf16),
         dk=pltpu.VMEM((2, s.line, s.mp), bf16), expand=pltpu.VMEM((s.long, s.line), bf16),
         dp_full=pltpu.VMEM((lanes, s.line), bf16), hc_full=pltpu.VMEM((lanes, ch), bf16),
-        legal_v=pltpu.VMEM((8, s.mp), jnp.int32), share=pltpu.VMEM((8, ch), f32),
+        legal_both=pltpu.VMEM((8, s.mp), jnp.int32),
     )
+    for name in ("w1", "w2", "gains", "shifts", "hc", "dense", "legal"):
+        scratch[name + "_v"] = pltpu.VMEM(inputs[name].shape, inputs[name].dtype)
+    for name in ("hng", "hns", "target"):
+        scratch[name + "_v"] = pltpu.SMEM(inputs[name].shape, inputs[name].dtype)
     if not s.fast:
         scratch["flat"] = pltpu.VMEM((9, ch, ch), f32)
         scratch["eight"] = pltpu.VMEM((9, 8, ch), f32)
@@ -831,11 +937,12 @@
         scratch["pb" + number] = pltpu.VMEM((s.nch, qn, gxn, s.crows, lanes), bf16)
         scratch["rp" + number] = pltpu.VMEM((s.nch, qn - 1, gxn, s.crows, lanes), bf16)
         scratch["zb" + number] = pltpu.VMEM((s.nch, gxn, s.crows, lanes), bf16)
+        scratch["rd" + number] = pltpu.VMEM((gxn * qn - 1, s.crows, lanes), bf16)
         scratch["rz" + number] = pltpu.VMEM((s.nch, gxn - 1, s.crows, lanes), bf16)
     run = pl.pallas_call(
         functools.partial(kernel, s, tuple(inputs), tuple(outputs), tuple(scratch)),
         out_shape=[jax.ShapeDtypeStruct(shape, kind) for shape, kind in outputs.values()],
-        in_specs=[pl.BlockSpec(memory_space=space) for _, space in inputs.values()],
+        in_specs=[pl.BlockSpec(memory_space=hbm) for _ in inputs],
         out_specs=[pl.BlockSpec(memory_space=hbm if n in ("out", "in_grad") else vmem) for n in outputs],
         scratch_shapes=list(scratch.values()),
         compiler_params=pltpu.CompilerParams(
@@ -844,13 +951,18 @@
         cost_estimate=pl.CostEstimate(flops=10_500_000_000, bytes_accessed=8_000_000, transcendentals=800_000),
         name="tower",
     )
-    results = run(*(value for value, _ in inputs.values()))
+    results = run(*inputs.values())
+    kinds = [jax.ShapeDtypeStruct(v.shape, v.dtype) for v in results]
+    out, in_grad, c1_grad, c2_grad, dense_grad, _ = kinds
+    small = [jax.ShapeDtypeStruct(v.shape, f32) for v in (gains, shifts, hc)]
+    loss, pair = (jax.ShapeDtypeStruct(shape, f32) for shape in ((1, 1), (2, 2)))
+    shapes = [out, loss, in_grad, c1_grad, c2_grad, *small, pair, jax.ShapeDtypeStruct(dense.shape, f32)]
     results = pl.pallas_call(
-        functools.partial(place, len(results)),
-        out_shape=[jax.ShapeDtypeStruct(v.shape, v.dtype) for v in results],
-        in_specs=[pl.BlockSpec(memory_space=hbm) for _ in results],
-        out_specs=[pl.BlockSpec(memory_space=hbm) for _ in results],
-        scratch_shapes=[pltpu.VMEM(v.shape, v.dtype) for v in results] + [dma((len(results),))] * 2,
+        functools.partial(place, s.w),
+        out_shape=shapes,
+        in_specs=[pl.BlockSpec(memory_space=hbm) for _ in kinds],
+        out_specs=[pl.BlockSpec(memory_space=hbm if n in (0, 2, 3, 4) else vmem) for n in range(len(shapes))],
+        scratch_shapes=[pltpu.VMEM(v.shape, v.dtype) for v in kinds] + [dma((len(kinds),))] * 2,
         name="place",
     )(*results)
     out, loss, in_grad, *rest = results

time: 91.1 us -> 83 us (0.911)
  Pallas kernels: 90.1 us -> 82.1 us
    pallas_call x2, Pallas kernels: 90.1 us -> 82.1 us  [the longest x1 79 us: body(): results = run(*inputs.values())]
where the time goes in v3:
time: 83 us; the launch traced here: 82.9 us
  Pallas kernels  82.1 us (99%)
    pallas_call x1, Pallas kernels, body(): results = run(*inputs.values())  79 us
    pallas_call x1, Pallas kernels, body(): pl.pallas_call(functools.partial(place, s.w), out_shape=shapes, in_specs=...  3.09 us

profile of v3, /device:TPU:0, one launch (start us, length us, event | category | flops | bytes accessed | tf_op | source)
XLA Modules:
  0.0 82.9 jit_solution(11055131685411847176)
XLA Ops:
  0.6 79.0 %tower.1 = (bf16[19,19,4,256]{3,2,1,0:T(4,128)(2,1)}, bf16[19,19,4,256]{3,2,1,0:T(4,128)(2,1)}, f32[9,8,256]{2,1,0:T(8,128)}, f32[9,8,256]{2,1,0:T(8,128)}, f32[32,384]{1,0:T(8,128)}, /*index=5*/f32[16,128]{1,0:T(8,128)}) custom-call(bf16[19,19,4,256]{3,2,1,0:T(4,128)(2,1)} %bitcast.5, bf16[9,8,256]{2,1,0:T(8,128)(2,1)} %refs_1_.1, ...), custom_call_target="tpu_custom_call" | custom-call | flops 10499999744 | bytes 8000000 | tf_op jit(solution)/shard_map/tower/pallas_call | solution.py:954
  79.6 3.1 %place.1 = (bf16[19,19,4,256]{3,2,1,0:T(4,128)(2,1)}, f32[1,1]{1,0:T(1,128)}, bf16[19,19,4,256]{3,2,1,0:T(4,128)(2,1)}, f32[9,8,256]{2,1,0:T(8,128)}, f32[9,8,25...) custom-call(bf16[19,19,4,256]{3,2,1,0:T(4,128)(2,1)} %get-tuple-elem, ...), custom_call_target="tpu_custom_call" | custom-call | tf_op jit(solution)/shard_map/place/pallas_call | solution.py:960

commit v4 on v3

--- a/solution.py
+++ b/solution.py
@@ -63,9 +63,9 @@
     s.wide = s.side + 1
     s.br = s.wide * s.nb
     s.rows = s.side * s.br
-    s.padded = s.rows + 2 * s.br
     s.line = up_to(s.side * s.wide, lanes)
-    s.long = up_to(s.rows, lanes)
+    s.long = up_to(s.rows, 3 * lanes)
+    s.padded = s.long + 2 * s.br
     s.cells = s.side * s.side
     s.moves = moves
     s.mp = up_to(moves, lanes)
@@ -148,7 +148,7 @@
 
     for planes in (r.x3, r.a3, r.d3):
         planes[0:br, :] = jnp.zeros((br, 3 * ch), bf16)
-        planes[s.padded - br :, :] = jnp.zeros((br, 3 * ch), bf16)
+        planes[br + s.rows :, :] = jnp.zeros((s.padded - br - s.rows, 3 * ch), bf16)
     inside = iota((br, ch), 0) < nb * s.side
 
     def store3(planes, i, block):
@@ -188,16 +188,25 @@
 
     units = [(r.s1, p) for p in range(s.nch)] + [(r.s2, p) for p in range(s.nch)] + [(r.sd, 0), (r.fd, 0)]
 
+    turned = {s.nch} if s.nch > 1 else set()
+
     def g_start(u):
         store, at = units[u][0], span(units[u])
         own = store.at[gx, q, c, at]
         for k in range(1, gxn):
-            send(own, own, r.g_sem.at[u, 0], r.g_sem.at[u, 5 + k], (z_peer(k), gy))
+            if u not in turned:
+                send(own, own, r.g_sem.at[u, 0], r.g_sem.at[u, 5 + k], (z_peer(k), gy))
         for j in range(qn - 1, 0, -1):
             send(own, own, r.g_sem.at[u, 1], r.g_sem.at[u, 4], (gx, 2 * q_peer(j) + c))
 
     def g_forward(u):
         store, at = units[u][0], span(units[u])
+        if u in turned:
+            take(r.g_sem.at[u, 4], store.at[gx, pl.ds(0, qn - 1), 0, at])
+            block = store.at[gx, :, c, at]
+            for k in range(gxn - 1, 0, -1):
+                send(block, block, r.g_sem.at[u, 2], r.g_sem.at[u, 5 + k], (z_peer(k), gy))
+            return
         for k in range(1, gxn):
             block = store.at[z_peer(k), q, c, at]
             take(r.g_sem.at[u, 5 + k], block)
@@ -206,7 +215,11 @@
 
     def g_cross(u):
         store, at = units[u][0], span(units[u])
-        take(r.g_sem.at[u, 4], store.at[:, pl.ds(0, qn - 1), 0, at])
+        if u in turned:
+            for k in range(1, gxn):
+                take(r.g_sem.at[u, 5 + k], store.at[z_peer(k), :, c, at])
+        else:
+            take(r.g_sem.at[u, 4], store.at[:, pl.ds(0, qn - 1), 0, at])
         block = store.at[:, :, c, at]
         send(block, block, r.g_sem.at[u, 3], r.g_sem.at[u, 5], other)
 
@@ -216,9 +229,12 @@
 
     def g_drain(u):
         store, at = units[u][0], span(units[u])
-        take(r.g_sem.at[u, 0], store.at[pl.ds(0, gxn - 1), 0, 0, at])
         take(r.g_sem.at[u, 1], store.at[0, pl.ds(0, qn - 1), 0, at])
-        take(r.g_sem.at[u, 2], store.at[pl.ds(0, gxn - 1), pl.ds(0, qn - 1), 0, at])
+        if u in turned:
+            take(r.g_sem.at[u, 2], store.at[pl.ds(0, gxn - 1), :, 0, at])
+        else:
+            take(r.g_sem.at[u, 0], store.at[pl.ds(0, gxn - 1), 0, 0, at])
+            take(r.g_sem.at[u, 2], store.at[pl.ds(0, gxn - 1), pl.ds(0, qn - 1), 0, at])
         take(r.g_sem.at[u, 3], store.at[:, :, 0, at])
 
     def shard_of(store, d):
@@ -422,9 +438,12 @@
     n1 = s.nch
     for u in range(n1):
         g_start(u)
+    for u in turned:
+        g_start(u)
     g_forward(0)
     for u in range(n1, 2 * n1):
-        g_start(u)
+        if u not in turned:
+            g_start(u)
     for u in range(1, 2 * n1):
         g_forward(u)
     g_start(2 * n1)
@@ -438,12 +457,19 @@
 
     def conv_part(planes, weight, di, out):
         v = dot(planes[br * di : br * di + s.rows, :], weight[di])
-        out[...] = v if di == 0 else out[...] + v
+        out[0 : s.rows, :] = v if di == 0 else out[0 : s.rows, :] + v
+
+    chunk = s.long // 3
 
     def conv(planes, weight, out):
-        v = dot(planes[0 : s.rows, :], weight[0])
-        v = v + dot(planes[br : br + s.rows, :], weight[1])
-        out[...] = v + dot(planes[2 * br : 2 * br + s.rows, :], weight[2])
+        def one(k, _):
+            at = pl.multiple_of(k * chunk, 16)
+            v = dot(planes[pl.ds(at, chunk), :], weight[0])
+            v = v + dot(planes[pl.ds(at + br, chunk), :], weight[1])
+            out[pl.ds(at, chunk), :] = v + dot(planes[pl.ds(at + 2 * br, chunk), :], weight[2])
+            return 0
+
+        lax.fori_loop(0, 3, one, 0)
 
     for part in range(n1):
         g_done(part)
@@ -460,10 +486,13 @@
     fetch["cot"].wait()
 
     def flip(weight, back):
-        for di in range(3):
-            for dj in range(3):
-                tap = weight[2 - di, (2 - dj) * ch : (3 - dj) * ch, :]
-                back[di, dj * ch : (dj + 1) * ch, :] = jnp.transpose(tap)
+        def one(n, _):
+            di, dj = lax.div(n, 3), lax.rem(n, 3)
+            tap = weight[2 - di, pl.ds(pl.multiple_of((2 - dj) * ch, ch), ch), :]
+            back[di, pl.ds(pl.multiple_of(dj * ch, ch), ch), :] = jnp.transpose(tap)
+            return 0
+
+        lax.fori_loop(0, 9, one, 0)
 
     for u in range(n1, 2 * n1):
         g_cross(u)
@@ -519,11 +548,7 @@
         place = jnp.where(wanted, shard * s.rp + (source - shard * s.rsh), -1)
         pick = (shard_rows == place).astype(f32).astype(bf16)
         r.dk[k] = dot(pick, dense_all).astype(bf16)
-    r.dp_full[...] = jnp.zeros_like(r.dp_full)
-    r.hc_full[...] = jnp.zeros_like(r.hc_full)
     row = iota((16, ch), 0)
-    both = jnp.where(row < nb, hc0, jnp.where(row < 2 * nb, hc1, 0.0))
-    r.hc_full[0:16, :] = both.astype(bf16)
     hc_rows = jnp.where(row == 0, hc0, jnp.where(row == 1, hc1, 0.0)).astype(bf16)
 
     x_wait(1, r.t2)
@@ -623,9 +648,11 @@
     def of_head(v, at):
         return jnp.where(iota((8, 1), 0) < nb, v[:, at : at + 1], v[:, at + 32 : at + 33])
 
+    mean_long = jnp.concatenate([mean_k[:, 0:1], mean_k[:, 32:33]], axis=0)
     mean_p = of_head(mean_k, 0)
     squares = of_head(squares, 0) + of_head(squares, 64)
     inv_p = lax.rsqrt(squares / s.count + epsilon)
+    inv_long = jnp.concatenate([inv_p[0:1], inv_p[nb : nb + 1]], axis=0)
     gain_p = jnp.where(iota((8, 1), 0) < nb, r.hng_v[0], r.hng_v[1])
     shift_p = jnp.where(iota((8, 1), 0) < nb, r.hns_v[0], r.hns_v[1])
     xhat_p = (p8 - mean_p) * inv_p
@@ -693,6 +720,18 @@
     r.fd[gx, q, c] = r.fd_own[...].astype(bf16)
     g_start(2 * n1 + 1)
     flip(r.wt2, r.wb2)
+    scaled_long = dnh_long * scale_p
+    dnh_heads = [jnp.sum(scaled_long[nb * k : nb * k + nb], axis=0, keepdims=True) for k in range(2)]
+    xhat_long = (p_long[0:2] - mean_long) * inv_long
+    xhat_long = jnp.where(valid_long[0:1], xhat_long, 0.0)
+    row = iota((16, s.long), 0)
+    terms_long = jnp.where(valid_long[0:1], 1.0, 0.0)
+    for n, value in ((0, dnh_heads[0]), (1, dnh_heads[1]), (3, xhat_long[0:1]), (4, xhat_long[1:2])):
+        terms_long = jnp.where(row == n, value, terms_long)
+    terms_long = jnp.where(row < 5, terms_long, 0.0)
+    r.terms[...] = terms_long.astype(bf16)
+    tall_terms = jnp.concatenate([terms_long, jnp.zeros((lanes - 16, s.long), f32)], axis=0)
+    r.terms_t[...] = jnp.transpose(tall_terms).astype(bf16)
     x_wait(4, r.t5)
     group_wait(7, r.tl)
     te = jnp.sum(r.tl[...], axis=0)
@@ -703,8 +742,6 @@
     first_lane = iota((1, lanes), 1) == 0
     r.tiny[1:2, :] = jnp.where(first_lane, *gain_sums)
     r.tiny[2:3, :] = jnp.where(first_lane, *shift_sums)
-    gain_sum = jnp.where(iota((8, 1), 0) < nb, *gain_sums)
-    shift_sum = jnp.where(iota((8, 1), 0) < nb, *shift_sums)
     g2s, s2s = t5[0:1], t5[1:2]
     for k in range(2):
         weight = (hc0, hc1)[k] * (scale_p[nb * k : nb * k + 1] / s.count)
@@ -712,15 +749,15 @@
         mean_k = mean_p[nb * k : nb * k + 1]
         s2s = s2s - weight * (shift_sums[k] * te[0:1] + gain_part * (te[k + 1 : k + 2] - mean_k * te[0:1]))
         g2s = g2s - weight * (shift_sums[k] * te[4:5] + gain_part * (te[k + 5 : k + 6] - mean_k * te[4:5]))
-    dp = scale_p * (dnh - (shift_sum + xhat_p * gain_sum) / s.count)
-    dp = jnp.where(valid, dp, 0.0)
-    r.dp_full[0:16, :] = tall(dp)
-
-    spread_p = dot_nt(r.expand[0 : s.rows, :], r.dp_full[...])
-    row, col = iota((s.rows, lanes), 0), iota((s.rows, lanes), 1)
-    spread_p = jnp.where((row & (nb - 1)) == (col & (nb - 1)), spread_p, 0.0).astype(bf16)
-    r.spread[...] = spread_p
-    r.up[...] = dot(spread_p, r.hc_full[...])
+    scales = [scale_p[nb * k : nb * k + 1] / s.count for k in range(2)]
+    ones_of = [shift_sums[k] * scales[k] for k in range(2)]
+    xhat_of = [gain_sums[k] * scales[k] for k in range(2)]
+
+    row = iota((lanes, ch), 0)
+    mix = jnp.where(row == 0, hc0, jnp.where(row == 1, hc1, 0.0))
+    mix = jnp.where(row == 2, -(hc0 * ones_of[0] + hc1 * ones_of[1]), mix)
+    mix = jnp.where(row == 3, -hc0 * xhat_of[0], jnp.where(row == 4, -hc1 * xhat_of[1], mix))
+    r.up[...] = dot(r.terms_t[...], mix.astype(bf16))
 
     def sums_back(field, xhat, carry):
         f = field.reshape(br // 8, 8, ch)
@@ -759,11 +796,11 @@
     r.st6[0:1, :] = jnp.sum(g1, axis=0, keepdims=True)
     r.st6[1:2, :] = jnp.sum(s1, axis=0, keepdims=True)
     x_send(5, r.st6, r.t6)
-    head_grad = lax.dot_general(
-        r.spread[...], r.out_r[0 : s.rows, :], (((0,), (0,)), ((), ())), preferred_element_type=f32
-    )
-    r.sth[0:1, :] = head_grad[0:1] + head_grad[1:2] + head_grad[2:3] + head_grad[3:4]
-    r.sth[1:2, :] = head_grad[4:5] + head_grad[5:6] + head_grad[6:7] + head_grad[7:8]
+    against_out = dot(r.terms[...], r.out_r[...])
+    for k in range(2):
+        r.sth[k : k + 1, :] = (
+            against_out[k : k + 1] - ones_of[k] * against_out[2:3] - xhat_of[k] * against_out[k + 3 : k + 4]
+        )
     x_send(6, r.sth, r.th)
     for part in range(early):
         rs_plane(rs2, part)
@@ -897,7 +934,7 @@
         dense_grad=((s.rp, s.mp), f32), tiny=((16, lanes), f32),
     )
     gxn, qn, n, ch = s.gx_n, s.q_n, s.n_dev, s.ch
-    field = pltpu.VMEM((s.rows, ch), f32)
+    field = pltpu.VMEM((s.long, ch), f32)
     boards = pltpu.VMEM((s.side, s.wide, s.nb, ch), bf16)
     planes = pltpu.VMEM((s.padded, 3 * ch), bf16)
     turned = pltpu.VMEM((ch, s.rows), bf16)
@@ -912,7 +949,7 @@
         stage=pltpu.VMEM((s.blk1, lanes), f32), small=pltpu.VMEM((8, lanes), f32),
         s1=pltpu.VMEM((gxn, qn, 2, s.blk1, lanes), bf16), s2=pltpu.VMEM((gxn, qn, 2, s.blk, lanes), bf16),
         sd=pltpu.VMEM((gxn, qn, 2, s.rp, s.mp), bf16), dense_f=pltpu.VMEM((s.rp, s.mp), f32),
-        x3=planes, a3=planes, d3=planes, out_r=pltpu.VMEM((s.long, ch), bf16), spread=pltpu.VMEM((s.rows, lanes), bf16),
+        x3=planes, a3=planes, d3=planes, out_r=pltpu.VMEM((s.long, ch), bf16), terms=pltpu.VMEM((16, s.long), bf16), terms_t=pltpu.VMEM((s.long, lanes), bf16),
         xt=turned, at=turned, wt1=weight, wt2=weight, wb1=weight, wb2=weight,
         pars=pltpu.VMEM((8, ch), f32), h1=field, h2=field, dz=field, back1=field, up=field,
         st1=two, t1=pltpu.VMEM((n, 2, ch), f32), st2=two, t2=pltpu.VMEM((n, 2, ch), f32),
@@ -921,7 +958,6 @@
         sth=two, th=pltpu.VMEM((n, 2, ch), f32), vu=pltpu.VMEM((s.long, 2 * ch), bf16),
         fd_own=pltpu.VMEM((16, s.line), f32), fd=pltpu.VMEM((gxn, qn, 2, 16, s.line), bf16),
         dk=pltpu.VMEM((2, s.line, s.mp), bf16), expand=pltpu.VMEM((s.long, s.line), bf16),
-        dp_full=pltpu.VMEM((lanes, s.line), bf16), hc_full=pltpu.VMEM((lanes, ch), bf16),
         legal_both=pltpu.VMEM((8, s.mp), jnp.int32),
     )
     for name in ("w1", "w2", "gains", "shifts", "hc", "dense", "legal"):

time: 83 us -> 79.3 us (0.955)
  Pallas kernels: 82.1 us -> 78.4 us
    pallas_call x1, Pallas kernels: 79 us -> 75.3 us  [body(): results = run(*inputs.values())]
where the time goes in v4:
time: 79.3 us; the launch traced here: 79.2 us
  Pallas kernels  78.4 us (99%)
  between operations  0.82 us (1%)
    pallas_call x1, Pallas kernels, body(): results = run(*inputs.values())  75.3 us
    pallas_call x1, Pallas kernels, body(): pl.pallas_call(functools.partial(place, s.w), out_shape=shapes, in_specs=...  3.09 us

profile of v4, /device:TPU:0, one launch (start us, length us, event | category | flops | bytes accessed | tf_op | source)
XLA Modules:
  0.0 79.2 jit_solution(5029274032041683719)
XLA Ops:
  0.6 75.3 %tower.1 = (bf16[19,19,4,256]{3,2,1,0:T(4,128)(2,1)}, bf16[19,19,4,256]{3,2,1,0:T(4,128)(2,1)}, f32[9,8,256]{2,1,0:T(8,128)}, f32[9,8,256]{2,1,0:T(8,128)}, f32[32,384]{1,0:T(8,128)}, /*index=5*/f32[16,128]{1,0:T(8,128)}) custom-call(bf16[19,19,4,256]{3,2,1,0:T(4,128)(2,1)} %bitcast.5, bf16[9,8,256]{2,1,0:T(8,128)(2,1)} %refs_1_.1, ...), custom_call_target="tpu_custom_call" | custom-call | flops 10499999744 | bytes 8000000 | tf_op jit(solution)/shard_map/tower/pallas_call | solution.py:990
  75.9 3.1 %place.1 = (bf16[19,19,4,256]{3,2,1,0:T(4,128)(2,1)}, f32[1,1]{1,0:T(1,128)}, bf16[19,19,4,256]{3,2,1,0:T(4,128)(2,1)}, f32[9,8,256]{2,1,0:T(8,128)}, f32[9,8,25...) custom-call(bf16[19,19,4,256]{3,2,1,0:T(4,128)(2,1)} %get-tuple-elem, ...), custom_call_target="tpu_custom_call" | custom-call | tf_op jit(solution)/shard_map/place/pallas_call | solution.py:996

commit v5 on v4

--- a/solution.py
+++ b/solution.py
@@ -561,12 +561,9 @@
         r.dz[at, :] = z
         a = jnp.where(inside, gelu(z), 0.0)
         r.out_r[at, :] = a.astype(bf16)
-        r.out_v[i] = to_board(a)
         return 0
 
     lax.fori_loop(0, s.side, act2, 0)
-    put_out = pltpu.make_async_copy(r.out_v, r.out, r.local_sem.at[len(names)])
-    put_out.start()
     p_long = dot_nt(hc_rows, r.out_r[...])[0:8]
     lane = iota((8, s.long), 1)
     lane_j = lane - divided(lane, br, s.long) * br
@@ -600,13 +597,17 @@
         scaled = slope * ((r.h2[at, :] - mean2) * inv2)
         r.vu[at, 0:ch] = slope.astype(bf16)
         r.vu[at, ch:] = scaled.astype(bf16)
+        r.out_v[i] = to_board(r.out_r[at, :].astype(f32))
         cot = from_board(r.cot_v[i])
+        r.cot_s[at, :] = cot * slope
         a = (cot * scaled).reshape(br // 8, 8, ch)
         b = (cot * slope).reshape(br // 8, 8, ch)
         return carry[0] + jnp.sum(a, axis=0), carry[1] + jnp.sum(b, axis=0)
 
     zero = jnp.zeros((8, ch), f32)
     cot_g, cot_s = lax.fori_loop(0, s.side, slope2, (zero, zero))
+    put_out = pltpu.make_async_copy(r.out_v, r.out, r.local_sem.at[len(names)])
+    put_out.start()
     cot_g, cot_s = jnp.sum(cot_g, axis=0, keepdims=True), jnp.sum(cot_s, axis=0, keepdims=True)
     row = iota((16, s.long), 0)
     centred = jnp.where(valid_long[0:1], p_long[0:2] - mean_row[0:2], 0.0)
@@ -767,7 +768,7 @@
     def to_field2(i, _):
         at = rows_of(i)
         xhat = (r.h2[at, :] - mean2) * inv2
-        dz = (from_board(r.cot_v[i]) + r.up[at, :]) * r.dz[at, :]
+        dz = r.cot_s[at, :] + r.up[at, :] * r.dz[at, :]
         r.dz[at, :] = dz
         d = (gain2 * inv2) * (dz - (s2s + xhat * g2s) * (1.0 / s.count))
         store3(r.d3, i, jnp.where(inside, d, 0.0))
@@ -776,8 +777,20 @@
     lax.fori_loop(0, s.side, to_field2, 0)
 
     def wgrad(planes_t, di):
-        start = 2 * br - br * di
-        return dot(planes_t[...], r.d3[start : start + s.rows, :])
+        start = pl.multiple_of(2 * br - br * di, 16)
+        return dot(planes_t[...], r.d3[pl.ds(start, s.rows), :])
+
+    def leave(planes_t, first, b):
+        def one(di, _):
+            rs_fill(di, wgrad(planes_t, di), b)
+            if s.fast:
+                rs_cross(b, di)
+            return 0
+
+        lax.fori_loop(first, 3, one, 0)
+        rs_fill_rest(b)
+        if not s.fast:
+            rs_cross(b, 0)
 
     early = 1 if s.fast else 0
     for di in range(early):
@@ -804,13 +817,7 @@
     x_send(6, r.sth, r.th)
     for part in range(early):
         rs_plane(rs2, part)
-    for di in range(early, 3):
-        rs_fill(di, wgrad(r.at, di), rs2)
-        if s.fast:
-            rs_cross(rs2, di)
-    rs_fill_rest(rs2)
-    if not s.fast:
-        rs_cross(rs2, 0)
+    leave(r.at, early, rs2)
     for part in range(early, s.nch - 1):
         rs_plane(rs2, part)
     g_cross(2 * n1 + 1)
@@ -827,16 +834,9 @@
 
     rs_plane(rs2, s.nch - 1)
     lax.fori_loop(0, s.side, to_field1, 0)
-    for di in range(3):
-        rs_fill(di, wgrad(r.xt, di), rs1)
-        if s.fast:
-            rs_cross(rs1, di)
-            if di:
-                rs_plane(rs1, di - 1)
-    rs_fill_rest(rs1)
-    if not s.fast:
-        rs_cross(rs1, 0)
-    rs_plane(rs1, s.nch - 1)
+    leave(r.xt, 0, rs1)
+    for part in range(s.nch):
+        rs_plane(rs1, part)
     conv(r.d3, r.wb1, r.h1)
     for part in range(s.nch):
         rs_line(rs2, part)
@@ -951,7 +951,7 @@
         sd=pltpu.VMEM((gxn, qn, 2, s.rp, s.mp), bf16), dense_f=pltpu.VMEM((s.rp, s.mp), f32),
         x3=planes, a3=planes, d3=planes, out_r=pltpu.VMEM((s.long, ch), bf16), terms=pltpu.VMEM((16, s.long), bf16), terms_t=pltpu.VMEM((s.long, lanes), bf16),
         xt=turned, at=turned, wt1=weight, wt2=weight, wb1=weight, wb2=weight,
-        pars=pltpu.VMEM((8, ch), f32), h1=field, h2=field, dz=field, back1=field, up=field,
+        pars=pltpu.VMEM((8, ch), f32), h1=field, h2=field, dz=field, back1=field, up=field, cot_s=field,
         st1=two, t1=pltpu.VMEM((n, 2, ch), f32), st2=two, t2=pltpu.VMEM((n, 2, ch), f32),
         st3=pltpu.VMEM((1, lanes), f32), t3=pltpu.VMEM((n, 1, lanes), f32), ste=eight, te=pltpu.VMEM((s.gy_n, 8, ch), f32), stl=eight, tl=pltpu.VMEM((gxn, 8, ch), f32),
         st5=pltpu.VMEM((3, ch), f32), t5=pltpu.VMEM((n, 3, ch), f32), st6=two, t6=pltpu.VMEM((n, 2, ch), f32),

time: 79.3 us -> 78.7 us (level)
  no operation moved by 1% of the time
where the time goes in v5:
time: 78.7 us; the launch traced here: 78.6 us
  Pallas kernels  77.9 us (99%)
    pallas_call x1, Pallas kernels, body(): results = run(*inputs.values())  74.8 us
    pallas_call x1, Pallas kernels, body(): pl.pallas_call(functools.partial(place, s.w), out_shape=shapes, in_specs=...  3.09 us

profile of v5, /device:TPU:0, one launch (start us, length us, event | category | flops | bytes accessed | tf_op | source)
XLA Modules:
  0.0 78.6 jit_solution(10599194804335581018)
XLA Ops:
  0.6 74.8 %tower.1 = (bf16[19,19,4,256]{3,2,1,0:T(4,128)(2,1)}, bf16[19,19,4,256]{3,2,1,0:T(4,128)(2,1)}, f32[9,8,256]{2,1,0:T(8,128)}, f32[9,8,256]{2,1,0:T(8,128)}, f32[32,384]{1,0:T(8,128)}, /*index=5*/f32[16,128]{1,0:T(8,128)}) custom-call(bf16[19,19,4,256]{3,2,1,0:T(4,128)(2,1)} %bitcast.5, bf16[9,8,256]{2,1,0:T(8,128)(2,1)} %refs_1_.1, ...), custom_call_target="tpu_custom_call" | custom-call | flops 10499999744 | bytes 8000000 | tf_op jit(solution)/shard_map/tower/pallas_call | solution.py:990
  75.5 3.1 %place.1 = (bf16[19,19,4,256]{3,2,1,0:T(4,128)(2,1)}, f32[1,1]{1,0:T(1,128)}, bf16[19,19,4,256]{3,2,1,0:T(4,128)(2,1)}, f32[9,8,256]{2,1,0:T(8,128)}, f32[9,8,25...) custom-call(bf16[19,19,4,256]{3,2,1,0:T(4,128)(2,1)} %get-tuple-elem, ...), custom_call_target="tpu_custom_call" | custom-call | tf_op jit(solution)/shard_map/place/pallas_call | solution.py:996

commit v6 on v5

--- a/solution.py
+++ b/solution.py
@@ -440,11 +440,10 @@
         g_start(u)
     for u in turned:
         g_start(u)
-    g_forward(0)
     for u in range(n1, 2 * n1):
         if u not in turned:
             g_start(u)
-    for u in range(1, 2 * n1):
+    for u in range(2 * n1):
         g_forward(u)
     g_start(2 * n1)
     row, col = iota((s.long, s.line), 0), iota((s.long, s.line), 1)
@@ -809,18 +808,19 @@
     r.st6[0:1, :] = jnp.sum(g1, axis=0, keepdims=True)
     r.st6[1:2, :] = jnp.sum(s1, axis=0, keepdims=True)
     x_send(5, r.st6, r.t6)
+    for part in range(early):
+        rs_plane(rs2, part)
+    leave(r.at, early, rs2)
+    for part in range(early, s.nch - 1):
+        rs_plane(rs2, part)
+    g_cross(2 * n1 + 1)
+    rs_plane(rs2, s.nch - 1)
     against_out = dot(r.terms[...], r.out_r[...])
     for k in range(2):
         r.sth[k : k + 1, :] = (
             against_out[k : k + 1] - ones_of[k] * against_out[2:3] - xhat_of[k] * against_out[k + 3 : k + 4]
         )
     x_send(6, r.sth, r.th)
-    for part in range(early):
-        rs_plane(rs2, part)
-    leave(r.at, early, rs2)
-    for part in range(early, s.nch - 1):
-        rs_plane(rs2, part)
-    g_cross(2 * n1 + 1)
     x_wait(5, r.t6)
     t6 = jnp.sum(r.t6[...], axis=0)
     g1s, s1s = t6[0:1], t6[1:2]
@@ -832,7 +832,6 @@
         store3(r.d3, i, jnp.where(inside, d, 0.0))
         return 0
 
-    rs_plane(rs2, s.nch - 1)
     lax.fori_loop(0, s.side, to_field1, 0)
     leave(r.xt, 0, rs1)
     for part in range(s.nch):
@@ -898,19 +897,24 @@
 def place(w, x_ref, in_x_ref, c1, c2, dense, tiny, *refs):
     (out, loss, in_grad, c1_out, c2_out, gains, shifts, hc, hng, dense_out), refs = refs[:10], refs[10:]
     (out_v, in_v, c1_v, c2_v, dense_v, tiny_v), (came, went) = refs[:6], refs[6:]
-    sources, held = (tiny, dense, c1, c2, x_ref, in_x_ref), (tiny_v, dense_v, c1_v, c2_v, out_v, in_v)
-    fetch = [pltpu.make_async_copy(a, b, came.at[i]) for i, (a, b) in enumerate(zip(sources, held))]
-    put = [
-        pltpu.make_async_copy(a, b, went.at[i])
-        for i, (a, b) in enumerate(((c1_v, c1_out), (c2_v, c2_out), (out_v, out), (in_v, in_grad)))
+    side = out.shape[0]
+    cuts = [(n * side // 2, (n + 1) * side // 2) for n in range(2)]
+    moves = [(x_ref, out_v, out), (in_x_ref, in_v, in_grad)]
+    moves = [tuple(v.at[pl.ds(a, b - a)] for v in move) for move in moves for a, b in cuts]
+    moves += [(c1, c1_v, c1_out), (c2, c2_v, c2_out)]
+    fetch = [pltpu.make_async_copy(a, b, came.at[n]) for n, (a, b, _) in enumerate(moves)]
+    put = [pltpu.make_async_copy(b, d, went.at[n]) for n, (_, b, d) in enumerate(moves)]
+    fetch += [
+        pltpu.make_async_copy(a, b, came.at[len(moves) + n])
+        for n, (a, b) in enumerate(((tiny, tiny_v), (dense, dense_v)))
     ]
     for copy in fetch:
         copy.start()
-    for i in range(4):
-        fetch[i + 2].wait()
-        put[i].start()
-    fetch[0].wait()
-    fetch[1].wait()
+    for n in range(len(moves)):
+        fetch[n].wait()
+        put[n].start()
+    fetch[-2].wait()
+    fetch[-1].wait()
     loss[...] = tiny_v[0:1, 0:1]
     hng[...] = tiny_v[1:3, 0:2]
     gains[...] = tiny_v[8:10, 0:w]
@@ -998,7 +1002,7 @@
         out_shape=shapes,
         in_specs=[pl.BlockSpec(memory_space=hbm) for _ in kinds],
         out_specs=[pl.BlockSpec(memory_space=hbm if n in (0, 2, 3, 4) else vmem) for n in range(len(shapes))],
-        scratch_shapes=[pltpu.VMEM(v.shape, v.dtype) for v in kinds] + [dma((len(kinds),))] * 2,
+        scratch_shapes=[pltpu.VMEM(v.shape, v.dtype) for v in kinds] + [dma((16,))] * 2,
         name="place",
     )(*results)
     out, loss, in_grad, *rest = results

time: 78.7 us -> 78.1 us (level)
  no operation moved by 1% of the time
where the time goes in v6:
time: 78.1 us; the launch traced here: 77.9 us
  Pallas kernels  77.2 us (99%)
    pallas_call x1, Pallas kernels, body(): results = run(*inputs.values())  74.2 us
    pallas_call x1, Pallas kernels, body(): pl.pallas_call(functools.partial(place, s.w), out_shape=shapes, in_specs=...  3.05 us

profile of v6, /device:TPU:0, one launch (start us, length us, event | category | flops | bytes accessed | tf_op | source)
XLA Modules:
  0.0 77.9 jit_solution(16203086560438118998)
XLA Ops:
  0.6 74.2 %tower.1 = (bf16[19,19,4,256]{3,2,1,0:T(4,128)(2,1)}, bf16[19,19,4,256]{3,2,1,0:T(4,128)(2,1)}, f32[9,8,256]{2,1,0:T(8,128)}, f32[9,8,256]{2,1,0:T(8,128)}, f32[32,384]{1,0:T(8,128)}, /*index=5*/f32[16,128]{1,0:T(8,128)}) custom-call(bf16[19,19,4,256]{3,2,1,0:T(4,128)(2,1)} %bitcast.5, bf16[9,8,256]{2,1,0:T(8,128)(2,1)} %refs_1_.1, ...), custom_call_target="tpu_custom_call" | custom-call | flops 10499999744 | bytes 8000000 | tf_op jit(solution)/shard_map/tower/pallas_call | solution.py:994
  74.8 3.1 %place.1 = (bf16[19,19,4,256]{3,2,1,0:T(4,128)(2,1)}, f32[1,1]{1,0:T(1,128)}, bf16[19,19,4,256]{3,2,1,0:T(4,128)(2,1)}, f32[9,8,256]{2,1,0:T(8,128)}, f32[9,8,25...) custom-call(bf16[19,19,4,256]{3,2,1,0:T(4,128)(2,1)} %get-tuple-elem, ...), custom_call_target="tpu_custom_call" | custom-call | tf_op jit(solution)/shard_map/place/pallas_call | solution.py:1000

commit v7 on v6

--- a/solution.py
+++ b/solution.py
@@ -458,7 +458,7 @@
         v = dot(planes[br * di : br * di + s.rows, :], weight[di])
         out[0 : s.rows, :] = v if di == 0 else out[0 : s.rows, :] + v
 
-    chunk = s.long // 3
+    chunk = s.long // 2
 
     def conv(planes, weight, out):
         def one(k, _):
@@ -468,7 +468,7 @@
             out[pl.ds(at, chunk), :] = v + dot(planes[pl.ds(at + 2 * br, chunk), :], weight[2])
             return 0
 
-        lax.fori_loop(0, 3, one, 0)
+        lax.fori_loop(0, 2, one, 0)
 
     for part in range(n1):
         g_done(part)

time: 78.1 us -> 77.7 us (level)
  no operation moved by 1% of the time
where the time goes in v7:
time: 77.7 us; the launch traced here: 77.6 us
  Pallas kernels  76.9 us (99%)
    pallas_call x1, Pallas kernels, body(): results = run(*inputs.values())  73.9 us
    pallas_call x1, Pallas kernels, body(): pl.pallas_call(functools.partial(place, s.w), out_shape=shapes, in_specs=...  3.05 us

profile of v7, /device:TPU:0, one launch (start us, length us, event | category | flops | bytes accessed | tf_op | source)
XLA Modules:
  0.0 77.6 jit_solution(15268446532997727465)
XLA Ops:
  0.6 73.9 %tower.1 = (bf16[19,19,4,256]{3,2,1,0:T(4,128)(2,1)}, bf16[19,19,4,256]{3,2,1,0:T(4,128)(2,1)}, f32[9,8,256]{2,1,0:T(8,128)}, f32[9,8,256]{2,1,0:T(8,128)}, f32[32,384]{1,0:T(8,128)}, /*index=5*/f32[16,128]{1,0:T(8,128)}) custom-call(bf16[19,19,4,256]{3,2,1,0:T(4,128)(2,1)} %bitcast.5, bf16[9,8,256]{2,1,0:T(8,128)(2,1)} %refs_1_.1, ...), custom_call_target="tpu_custom_call" | custom-call | flops 10499999744 | bytes 8000000 | tf_op jit(solution)/shard_map/tower/pallas_call | solution.py:994
  74.5 3.1 %place.1 = (bf16[19,19,4,256]{3,2,1,0:T(4,128)(2,1)}, f32[1,1]{1,0:T(1,128)}, bf16[19,19,4,256]{3,2,1,0:T(4,128)(2,1)}, f32[9,8,256]{2,1,0:T(8,128)}, f32[9,8,25...) custom-call(bf16[19,19,4,256]{3,2,1,0:T(4,128)(2,1)} %get-tuple-elem, ...), custom_call_target="tpu_custom_call" | custom-call | tf_op jit(solution)/shard_map/place/pallas_call | solution.py:1000
